TPU v7x, 32 devices: a whole 2x2x4 slice. The times are simulated.
32 devices in a mesh: seq: 8 (over z, x), tp: 4 (over y, core).
Axes of the slice: x: 2, y: 2, z: 4, core: 2. Of those that a mesh axis runs over, the one named last changes fastest.
Arguments:
- resp_rows: bfloat16 [128, 16, 5120], P('seq', None, 'tp'), may hold values from -6 to 6
- resp_len: int32 [128], replicated, may hold values from 1 to 16, as said below
- resp_shard: int32 [128, 1], replicated, may hold values from 0 to 7; in each aligned block of 16 rows (0 to 15, 16 to 31, ...) at most 2 rows name the same one
- group_prompt: int32 [8], replicated, may hold values from 0 to 7, each once
- prompt_kv: bfloat16 [2, 8, 256, 1024], P(None, 'seq', None, 'tp'), may hold values from -72 to 72
- w_query: bfloat16 [5120, 3072], P(None, 'tp'), may hold values from -0.078125 to 0.078125
- w_keyval: bfloat16 [2, 5120, 1024], P(None, None, 'tp'), may hold values from -0.078125 to 0.078125
- w_out: bfloat16 [3072, 5120], P('tp'), may hold values from -0.109375 to 0.109375
Outputs:
- attended: bfloat16 [128, 16, 5120], P('seq', None, 'tp')
Inputs may be any that keep to these rules, and one draw needn't show every extreme that they name: `resp_shard`: in the rows of one device (one group) no learner appears more than 2 times, a bound that some block reaches. `group_prompt`: each prompt is answered by exactly one group. `resp_len`: some response has the full 16 tokens.
All inputs are finite; a program needn't handle non-finite values.
Results may differ from a plain program's by a relative error of at most 0.018.
Values may be sent and summed in bfloat16 or wider, within the bound.
A program may use at most 128 MiB of HBM per device.

v0:
```python
import math

import jax
import jax.numpy as jnp
from jax import lax
from jax.sharding import PartitionSpec as P

HD = 128
PL = 256


ROPE_BASE = 1000000.0


def rope_tables(count, width, offset):
    places = (offset + jnp.arange(count)).astype(jnp.float32)
    freqs = ROPE_BASE ** (-(jnp.arange(width // 2).astype(jnp.float32) * 2.0 / width))
    angles = places[:, None] * freqs[None, :]
    return (jnp.cos(angles), jnp.sin(angles))


def rotate(values, cosine, sine):
    half = values.shape[-1] // 2
    first = values[..., :half]
    second = values[..., half:]
    cosine = cosine[:, None, :]
    sine = sine[:, None, :]
    return jnp.concatenate([first * cosine - second * sine, second * cosine + first * sine], -1)


def attend(queries, own_keys, own_values, cached_keys, cached_values, lengths):
    scale = 1.0 / math.sqrt(queries.shape[-1])
    prior = (
        jnp.einsum("stkrh,spkh->skrtp", queries, cached_keys, preferred_element_type=jnp.float32)
        * scale
    )
    recent = (
        jnp.einsum("stkrh,sukh->skrtu", queries, own_keys, preferred_element_type=jnp.float32)
        * scale
    )
    places = jnp.arange(queries.shape[1])
    causal = places[:, None] >= places[None, :]
    recent = jnp.where(causal, recent, -1e30)
    top = jnp.maximum(jnp.max(prior, -1), jnp.max(recent, -1))
    prior_exp = jnp.exp(prior - top[..., None])
    recent_exp = jnp.exp(recent - top[..., None])
    total = jnp.sum(prior_exp, -1) + jnp.sum(recent_exp, -1)
    prior_w = (prior_exp / total[..., None]).astype(jnp.bfloat16)
    recent_w = (recent_exp / total[..., None]).astype(jnp.bfloat16)
    mixed = jnp.einsum(
        "skrtp,spkh->stkrh", prior_w, cached_values, preferred_element_type=jnp.float32
    )
    mixed = mixed + jnp.einsum(
        "skrtu,sukh->stkrh", recent_w, own_values, preferred_element_type=jnp.float32
    )
    valid = places[None, :] < lengths[:, None]
    mixed = jnp.where(valid[:, :, None, None, None], mixed, 0.0)
    return mixed.astype(jnp.bfloat16).reshape(queries.shape[0], queries.shape[1], -1)


def choose(match, capacity):
    group_size = match.shape[1]
    rank = jnp.cumsum(match.astype(jnp.int32), axis=1) - 1
    picked = match[:, None, :] & (rank[:, None, :] == jnp.arange(capacity)[None, :, None])
    chosen = jnp.sum(jnp.where(picked, jnp.arange(group_size)[None, None, :], 0), -1)
    filled = jnp.any(picked, -1)
    return (chosen.reshape(-1), filled.reshape(-1))


def per_device(resp_rows, resp_len, resp_shard, group_prompt, prompt_kv, w_query, w_keyval, w_out):
    learners = lax.axis_size("seq")
    learner = lax.axis_index("seq")
    group_size = resp_rows.shape[0]
    capacity = (group_size + learners - 1) // learners
    table = resp_shard[:, 0].reshape(learners, group_size)
    own_targets = lax.dynamic_slice_in_dim(table, learner, 1, 0)[0]
    send_pick, send_filled = choose(own_targets[None, :] == jnp.arange(learners)[:, None], capacity)
    recv_pick, recv_filled = choose(table == learner, capacity)
    sources = jnp.repeat(jnp.arange(learners), capacity)
    slot_lengths = jnp.where(recv_filled, resp_len[sources * group_size + recv_pick], 0)
    prompts = group_prompt[sources]
    whole_rows = lax.all_gather(resp_rows, "tp", axis=2, tiled=True)
    taken = jnp.take(whole_rows, send_pick, axis=0)
    features = lax.all_to_all(
        jnp.where(send_filled[:, None, None], taken, jnp.zeros_like(taken)),
        "seq",
        split_axis=0,
        concat_axis=0,
        tiled=True,
    )
    caches = lax.all_gather(prompt_kv, "seq", axis=1, tiled=True)
    slot_cache = jnp.take(caches, prompts, axis=1)
    slots, token_count, width = features.shape
    flat = features.reshape(slots * token_count, width)
    kv_local = w_keyval.shape[2] // HD
    q_local = w_query.shape[1] // HD
    ratio = q_local // kv_local
    cosine, sine = rope_tables(token_count, HD, PL)
    queries = jnp.dot(flat, w_query, preferred_element_type=jnp.float32).reshape(
        slots, token_count, q_local, HD
    )
    queries = (
        rotate(queries, cosine, sine)
        .astype(jnp.bfloat16)
        .reshape(slots, token_count, kv_local, ratio, HD)
    )
    projected = jnp.einsum("nd,cde->cne", flat, w_keyval, preferred_element_type=jnp.float32)
    keys = rotate(projected[0].reshape(slots, token_count, kv_local, HD), cosine, sine).astype(
        jnp.bfloat16
    )
    values = projected[1].astype(jnp.bfloat16).reshape(slots, token_count, kv_local, HD)
    prompt_len = slot_cache.shape[2]
    cached_keys = slot_cache[0].reshape(slots, prompt_len, kv_local, HD)
    cached_values = slot_cache[1].reshape(slots, prompt_len, kv_local, HD)
    attn = attend(queries, keys, values, cached_keys, cached_values, slot_lengths)
    partial_value = jnp.dot(
        attn.reshape(-1, q_local * HD), w_out, preferred_element_type=jnp.float32
    ).astype(jnp.bfloat16)
    partial_value = (
        lax.optimization_barrier(partial_value).astype(jnp.float32).reshape(slots, token_count, -1)
    )
    summed = lax.psum_scatter(
        partial_value.astype(jnp.bfloat16), "tp", scatter_dimension=2, tiled=True
    )
    return summed


def solution(mesh):
    return jax.shard_map(
        per_device,
        mesh=mesh,
        in_specs=(
            P("seq", None, "tp"),
            P(),
            P(),
            P(),
            P(None, "seq", None, "tp"),
            P(None, "tp"),
            P(None, None, "tp"),
            P("tp", None),
        ),
        out_specs=P("seq", None, "tp"),
        check_vma=False,
    )
```

profile of v0, /device:TPU:0, one launch (start us, length us, event | category | flops | bytes accessed | tf_op | source)
XLA Modules:
  0.0 216.8 jit_solution(12605469068936996471)
XLA Ops:
  7.4 0.7 all-gather.5.cloned.1.call-update
  8.6 1.3 reduce.3
  11.0 27.1 %all-gather.5.cloned.1.call-done = bf16[16,16,5120]{2,1,0:T(8,128)(2,1)} async-done(((bf16[16,16,1280]{2,1,0:T(8,128)(2,1)}), bf16[16,16,5120]{2,1,0:T(8,128)(2,1)}) %all-gather.5.cloned.1.call-update) | async-done | bytes 2621456 | tf_op jit(solution)/shard_map/all_gather | solution.py:82
  38.1 2.5 %gather_fusion.3 = bf16[16,16,5120]{2,1,0:T(8,128)(2,1)S(1)} fusion(bf16[16,16,5120]{2,1,0:T(8,128)(2,1)} %all-gather.5.cloned.1.call-done, s32[1024]{0:T(1024)S(1)} %pad_clamp_fusion), kind=kCustom, calls=%fused_computation.3 | custom fusion | bytes 5242944 | tf_op jit(solution)/shard_map/jit(_take)/gather | solution.py:83
  40.5 1.8 select_select_fusion
  42.4 5.5 %all-to-all-start = ((bf16[16,16,5120]{2,1,0:T(8,128)(2,1)}), bf16[16,16,5120]{2,1,0:T(8,128)(2,1)}, u32[]{:S(2)}, u32[]{:S(2)}) async-start(bf16[16,16,5120]{2,1,0:T(8,128)(2,1)} %select_select_fusion), calls=%async_computation | async-start | bytes 5242880 | tf_op jit(solution)/shard_map/all_to_all | solution.py:84
  48.5 10.6 %copy.39 = bf16[5120,768]{0,1:T(8,128)(2,1)} copy(bf16[5120,768]{1,0:T(8,128)(2,1)} %param.13) | data formatting | bytes 15728640 | tf_op args[5]
  60.1 0.7 gather_fusion.1
  60.8 0.7 gather_fusion
  61.8 67.3 %all-gather.3.cloned.1.call-done = bf16[2,8,256,256]{3,2,1,0:T(8,128)(2,1)} async-done(((bf16[2,1,256,256]{3,2,1,0:T(8,128)(2,1)}), bf16[2,8,256,256]{3,2,1,0:T(8,128)(2,1)}) %all-gather.3.cloned.1.call-update) | async-done | bytes 2097168 | tf_op jit(solution)/shard_map/all_gather | solution.py:91
  129.1 4.4 %gather_fusion.2 = bf16[16,2,256,256]{3,2,1,0:T(8,128)(2,1)} fusion(bf16[2,8,256,256]{3,2,1,0:T(8,128)(2,1)} %all-gather.3.cloned.1.call-done, s32[1024]{0:T(1024)S(1)} %pad_clamp_fusion.1), kind=kCustom, calls=%fused_computation.2 | custom fusion | bytes 8388672 | tf_op jit(solution)/shard_map/jit(_take)/gather | solution.py:92
  133.5 2.6 %select_bitcast_fusion = bf16[2,16,256,256]{3,2,0,1:T(8,128)(2,1)S(1)} fusion(bf16[16,2,256,256]{3,2,1,0:T(8,128)(2,1)} %gather_fusion.2, pred[16]{0:T(512)(128)(4,1)S(1)} %compare_and_fusion.1), kind=kLoop, calls=%fused_computation.5 | loop fusion | flops 2097152 | bytes 8388624 | tf_op jit(solution)/shard_map/jit(_take)/select_n | solution.py:92
  136.2 2.3 %fusion.27 = (bf16[1,16,256,256]{3,2,0,1:T(8,128)(2,1)}, bf16[1,16,256,256]{3,2,0,1:T(8,128)(2,1)}) fusion(bf16[2,16,256,256]{3,2,0,1:T(8,128)(2,1)S(1)} %select_bitcast_fusion), kind=kLoop, calls=%fused_computation.78 | loop fusion | bytes 8388608 | tf_op jit(solution)/shard_map/slice | solution.py:114
  138.5 2.8 %copy.35 = bf16[1,16,256,256]{2,3,1,0:T(8,128)(2,1)S(1)} copy(bf16[1,16,256,256]{3,2,0,1:T(8,128)(2,1)} %get-tuple-element.8) | data formatting | bytes 4194304 | tf_op jit(solution)/shard_map/slice | solution.py:113
  141.3 3.9 %copy.34 = bf16[1,16,256,256]{2,3,1,0:T(8,128)(2,1)} copy(bf16[1,16,256,256]{3,2,0,1:T(8,128)(2,1)} %get-tuple-element.7) | data formatting | bytes 4194304 | tf_op jit(solution)/shard_map/slice | solution.py:114
  145.3 4.8 %convolution_bitcast_fusion = f32[2,256,256]{2,1,0:T(8,128)S(1)} fusion(bf16[256,5120,1]{1,0,2:T(8,128)(2,1)} %bitcast.20, bf16[2,5120,256]{2,1,0:T(8,128)(2,1)} %param.14), kind=kOutput, calls=%fused_computation.21 | convolution fusion | flops 1342177280 | bytes 8388608 | tf_op jit(solution)/shard_map/nd,cde->cne/dot_general | solution.py:107
  150.6 6.1 %fusion = f32[16,16,6,128]{3,1,2,0:T(8,128)S(1)} fusion(bf16[6,128,5120,1]{2,1,0,3:T(8,128)(2,1)} %bitcast.75, bf16[16,16,5120]{2,1,0:T(8,128)(2,1)} %all-to-all-done), kind=kOutput, calls=%fused_computation.6 | convolution fusion | flops 2013265920 | bytes 11272192 | tf_op jit(solution)/shard_map/dot_general | solution.py:99
  157.1 0.6 bitcast_reduce_fusion
  157.7 1.0 fusion.29
  159.1 0.6 fusion.3
  160.1 1.0 copy-done.4
  161.1 2.6 %fusion.8 = bf16[16,16,2,3,128]{4,1,3,2,0:T(8,128)(2,1)S(1)} fusion(f32[16,2,128,3,16]{2,4,3,1,0:T(8,128)S(1)} %fusion.11, bf16[16,256,2,128,1]{1,3,4,2,0:T(8,128)(2,1)} %bitcast.81, f32[16,2,256,16,3]{2,3,4,1,0:T(8,128)S(1)} %copy-done.4, f32[16,2,3,16]{3,2,1,0:T(4,128)S(1)} %add.124, f32[16,2,3,16]{3,2,1,0:T(4,128)S(1)} %max.7, ...), kind=kOutput, calls=%fused_computation.22 | convolution fusion | flops 102432768 | bytes 4862208 | tf_op jit(solution)/shard_map/skrtp,spkh->stkrh/dot_general | solution.py:50
  164.3 7.0 %convolution_convert_fusion = bf16[256,5120]{1,0:T(8,128)(2,1)} fusion(bf16[256,768]{1,0:T(8,128)(2,1)S(1)} %reshape_reshape.3, bf16[768,5120]{1,0:T(8,128)(2,1)} %param.15), kind=kOutput, calls=%fused_computation.4 | convolution fusion | flops 2014576640 | bytes 10878976 | tf_op jit(solution)/shard_map/dot_general | solution.py:116
  171.3 38.0 %reduce-scatter.2.cloned.1.call-done = bf16[16,16,1280]{2,1,0:T(8,128)(2,1)} async-done(((bf16[16,16,5120]{2,1,0:T(8,128)(2,1)}), bf16[16,16,1280]{2,1,0:T(8,128)(2,1)}) %reduce-scatter.2.cloned.1.call-update) | async-done | bytes 655376 | tf_op jit(solution)/shard_map/reduce_scatter | solution.py:122
  (66 shorter events, 5.5 us)
Async XLA Ops:
  7.4 52.8 %copy-start = (s32[8]{0:T(128)S(1)}, s32[8]{0:T(128)}, u32[]{:S(2)}) copy-start(s32[8]{0:T(128)} %param.11) | copy-start | bytes 100
  7.4 30.7 %all-gather.5.cloned.1.call-start = ((), (), s32[]{:S(2)}) async-start(), calls=%async_computation.3 | async-start | bytes 3276800 | tf_op jit(solution)/shard_map/all_gather | solution.py:82
  42.4 102.9 %all-to-all-start = ((bf16[16,16,5120]{2,1,0:T(8,128)(2,1)}), bf16[16,16,5120]{2,1,0:T(8,128)(2,1)}, u32[]{:S(2)}, u32[]{:S(2)}) async-start(bf16[16,16,5120]{2,1,0:T(8,128)(2,1)} %select_select_fusion), calls=%async_computation | async-start | bytes 5242880 | tf_op jit(solution)/shard_map/all_to_all | solution.py:84
  47.9 81.2 %all-gather.3.cloned.1.call-start = ((), (), s32[]{:S(2)}) async-start(), calls=%async_computation.2 | async-start | bytes 2359296 | tf_op jit(solution)/shard_map/all_gather | solution.py:91
  48.5 12.3 %copy-start.2 = (s32[128]{0:T(128)S(1)}, s32[128]{0:T(128)}, u32[]{:S(2)}) copy-start(s32[128]{0:T(128)} %param.9) | copy-start | bytes 1540
  48.5 160.8 %reduce-scatter.2.cloned.1.call-start = ((), (), s32[]{:S(2)}) async-start(), calls=%async_computation.4 | async-start | bytes 3276800 | tf_op jit(solution)/shard_map/reduce_scatter | solution.py:122
  157.7 1.3 copy-start.3
  159.7 1.4 copy-start.4
  164.3 45.1 %copy-start.1 = (s32[8]{0:T(128)S(1)}, s32[8]{0:T(128)}, u32[]{:S(2)}) copy-start(s32[8]{0:T(128)} %param.11) | copy-start | bytes 100
Sparse Core Ops, SparseCore 0:
  9.8 28.2 all-gather.4
  171.4 37.8 reduce-scatter.1
Sparse Core Ops, SparseCore 1:
  50.6 78.5 all-gather.2
where the time goes:
time: 218 us; the launch traced here: 217 us
  waiting for transfers between devices  134 us (61%)
  local copies, waits for them, and re-layouts  31.5 us (14%)
  matrix products  22.4 us (10%)
  between operations  15.1 us (7%)
  other arithmetic  8.37 us (4%)
  starting transfers between devices  5.59 us (3%)
    all_gather x1, waiting for transfers between devices, per_device(): caches = lax.all_gather(prompt_kv, 'seq', axis=1, tiled=True)  67.3 us
    reduce_scatter x1, waiting for transfers between devices, per_device(): lax.psum_scatter(partial_value.astype(jnp.bfloat16), 'tp', scatter_dimens...  38 us
    all_gather x1, waiting for transfers between devices, per_device(): whole_rows = lax.all_gather(resp_rows, 'tp', axis=2, tiled=True)  27.1 us
    unnamed x12, local copies, waits for them, and re-layouts  12.2 us
    dot_general x1, matrix products, per_device(): jnp.dot(attn.reshape(-1, q_local * HD), w_out, preferred_element_type=jnp...  6.99 us
    slice x2, local copies, waits for them, and re-layouts, per_device(): cached_values = slot_cache[1].reshape(slots, prompt_len, kv_local, HD)  6.21 us
    dot_general x1, matrix products, per_device(): jnp.dot(flat, w_query, preferred_element_type=jnp.float32)  6.05 us
    all_to_all x1, starting transfers between devices, per_device(): lax.all_to_all(jnp.where(send_filled[:, None, None], taken, jnp.zeros_lik...  5.51 us
  transfers between devices with their start and end apart: 4, of which 3 were waited for; matrix products, arithmetic and copies ran while one was open for 15% of the time, Pallas kernels for 0%

commit v1 on v0

v1 whole, which is shorter than its diff:
```python
import math

import jax
import jax.numpy as jnp
from jax import lax
from jax.sharding import PartitionSpec as P

HD = 128
PL = 256


ROPE_BASE = 1000000.0


def rope_tables(count, width, offset):
    places = (offset + jnp.arange(count)).astype(jnp.float32)
    freqs = ROPE_BASE ** (-(jnp.arange(width // 2).astype(jnp.float32) * 2.0 / width))
    angles = places[:, None] * freqs[None, :]
    return (jnp.cos(angles), jnp.sin(angles))


def rotate(values, cosine, sine):
    half = values.shape[-1] // 2
    first = values[..., :half]
    second = values[..., half:]
    cosine = cosine[:, None, :]
    sine = sine[:, None, :]
    return jnp.concatenate([first * cosine - second * sine, second * cosine + first * sine], -1)


def attend(queries, own_keys, own_values, cached_keys, cached_values, lengths):
    scale = 1.0 / math.sqrt(queries.shape[-1])
    prior = (
        jnp.einsum("stkrh,pkh->krstp", queries, cached_keys, preferred_element_type=jnp.float32)
        * scale
    )
    recent = (
        jnp.einsum("stkrh,sukh->krstu", queries, own_keys, preferred_element_type=jnp.float32)
        * scale
    )
    places = jnp.arange(queries.shape[1])
    causal = places[:, None] >= places[None, :]
    recent = jnp.where(causal, recent, -1e30)
    top = jnp.maximum(jnp.max(prior, -1), jnp.max(recent, -1))
    prior_exp = jnp.exp(prior - top[..., None])
    recent_exp = jnp.exp(recent - top[..., None])
    total = jnp.sum(prior_exp, -1) + jnp.sum(recent_exp, -1)
    prior_w = (prior_exp / total[..., None]).astype(jnp.bfloat16)
    recent_w = (recent_exp / total[..., None]).astype(jnp.bfloat16)
    mixed = jnp.einsum(
        "krstp,pkh->stkrh", prior_w, cached_values, preferred_element_type=jnp.float32
    )
    mixed = mixed + jnp.einsum(
        "krstu,sukh->stkrh", recent_w, own_values, preferred_element_type=jnp.float32
    )
    valid = places[None, :] < lengths[:, None]
    mixed = jnp.where(valid[:, :, None, None, None], mixed, 0.0)
    return mixed.astype(jnp.bfloat16).reshape(queries.shape[0], queries.shape[1], -1)


def choose(match, capacity):
    group_size = match.shape[1]
    rank = jnp.cumsum(match.astype(jnp.int32), axis=1) - 1
    picked = match[:, None, :] & (rank[:, None, :] == jnp.arange(capacity)[None, :, None])
    chosen = jnp.sum(jnp.where(picked, jnp.arange(group_size)[None, None, :], 0), -1)
    filled = jnp.any(picked, -1)
    return (chosen.reshape(-1), filled.reshape(-1))


def outgoing(resp_len, resp_shard, group_size):
    learners = lax.axis_size("seq")
    group = lax.axis_index("seq")
    capacity = (group_size + learners - 1) // learners
    own = lax.dynamic_slice_in_dim(resp_shard[:, 0], group * group_size, group_size, 0)
    pick, filled = choose(own[None, :] == jnp.arange(learners)[:, None], capacity)
    lengths = jnp.where(filled, resp_len[group * group_size + pick], 0)
    return pick, lengths


def per_device(resp_rows, resp_len, resp_shard, group_prompt, prompt_kv, w_query, w_keyval, w_out):
    group = lax.axis_index("seq")
    pick, lengths = outgoing(resp_len, resp_shard, resp_rows.shape[0])
    caches = lax.all_gather(prompt_kv, "seq", axis=1, tiled=True)
    cache = lax.dynamic_index_in_dim(caches, group_prompt[group], 1, keepdims=False)
    features = lax.all_gather(jnp.take(resp_rows, pick, axis=0), "tp", axis=2, tiled=True)
    slots, token_count, width = features.shape
    flat = features.reshape(slots * token_count, width)
    kv_local = w_keyval.shape[2] // HD
    q_local = w_query.shape[1] // HD
    ratio = q_local // kv_local
    cosine, sine = rope_tables(token_count, HD, PL)
    queries = jnp.dot(flat, w_query, preferred_element_type=jnp.float32).reshape(
        slots, token_count, q_local, HD
    )
    queries = (
        rotate(queries, cosine, sine)
        .astype(jnp.bfloat16)
        .reshape(slots, token_count, kv_local, ratio, HD)
    )
    keys = jnp.dot(flat, w_keyval[0], preferred_element_type=jnp.float32)
    keys = rotate(keys.reshape(slots, token_count, kv_local, HD), cosine, sine)
    keys = keys.astype(jnp.bfloat16)
    values = jnp.dot(flat, w_keyval[1], preferred_element_type=jnp.float32).astype(jnp.bfloat16)
    values = values.reshape(slots, token_count, kv_local, HD)
    cached_keys = cache[0].reshape(-1, kv_local, HD)
    cached_values = cache[1].reshape(-1, kv_local, HD)
    attn = attend(queries, keys, values, cached_keys, cached_values, lengths)
    partial_value = jnp.dot(
        attn.reshape(-1, q_local * HD), w_out, preferred_element_type=jnp.float32
    ).astype(jnp.bfloat16)
    summed = lax.psum_scatter(
        partial_value.reshape(slots, token_count, -1), "tp", scatter_dimension=2, tiled=True
    )
    return lax.all_to_all(summed, "seq", split_axis=0, concat_axis=0, tiled=True)


def solution(mesh):
    return jax.shard_map(
        per_device,
        mesh=mesh,
        in_specs=(
            P("seq", None, "tp"),
            P(),
            P(),
            P(),
            P(None, "seq", None, "tp"),
            P(None, "tp"),
            P(None, None, "tp"),
            P("tp", None),
        ),
        out_specs=P("seq", None, "tp"),
        check_vma=False,
    )
```

time: 218 us -> 174 us (0.80)
  waiting for transfers between devices: 134 us -> 89.9 us
  blocking collectives: 0 us -> 23.2 us
  local copies, waits for them, and re-layouts: 31.5 us -> 24 us
  starting transfers between devices: 5.59 us -> 0.09 us
  other arithmetic: 8.37 us -> 3.01 us
  matrix products: 22.4 us -> 17.6 us
    all_gather x1, waiting for transfers between devices: 67.3 us -> 31 us  [per_device(): caches = lax.all_gather(prompt_kv, 'seq', axis=1, tiled=True)]
    all_to_all x0 -> x1, blocking collectives: none -> 23.2 us  [per_device(): lax.all_to_all(summed, 'seq', split_axis=0, concat_axis=0, tiled=True)]
    slice x6 -> x1, local copies, waits for them, and re-layouts: 9.43 us -> 1.63 us  [per_device(): cached_values = cache[1].reshape(-1, kv_local, HD)]
    gather x4 -> x2, local copies, waits for them, and re-layouts: 8.21 us -> 1.25 us  [the longest x1 0.66 us: outgoing(): lengths = jnp.where(filled, resp_len[group * group_size + pick], 0)]
    all_to_all x1 -> x0, starting transfers between devices: 5.51 us -> none  [per_device(): lax.all_to_all(jnp.where(send_filled[:, None, None], taken, jnp.zeros_lik...]
    dot_general x5 -> x6, matrix products: 9.4 us -> 4.51 us  [the longest x1 1.02 us: attend(): jnp.einsum('stkrh,sukh->krstu', queries, own_keys, preferred_element_type...]
    dot_general x0 -> x2, local copies, waits for them, and re-layouts: none -> 4.78 us  [per_device(): keys = jnp.dot(flat, w_keyval[0], preferred_element_type=jnp.float32)]
    select_n x6 -> x3, other arithmetic: 4.51 us -> 0.98 us  [the longest x1 0.96 us: per_device(): jnp.take(resp_rows, pick, axis=0)]
  transfers between devices with their start and end apart: 4 -> 3, of which waited for: 3 -> 3; matrix products, arithmetic and copies ran while one was open for 15% -> 13% of each run, Pallas kernels for 0% -> 0%
where the time goes in v1:
time: 174 us; the launch traced here: 173 us
  waiting for transfers between devices  89.9 us (52%)
  local copies, waits for them, and re-layouts  24 us (14%)
  blocking collectives  23.2 us (13%)
  matrix products  17.6 us (10%)
  between operations  15.2 us (9%)
  other arithmetic  3.01 us (2%)
    reduce_scatter x1, waiting for transfers between devices, per_device(): lax.psum_scatter(partial_value.reshape(slots, token_count, -1), 'tp', sca...  34.8 us
    all_gather x1, waiting for transfers between devices, per_device(): caches = lax.all_gather(prompt_kv, 'seq', axis=1, tiled=True)  31 us
    all_gather x1, waiting for transfers between devices, per_device(): lax.all_gather(jnp.take(resp_rows, pick, axis=0), 'tp', axis=2, tiled=True)  24 us
    all_to_all x1, blocking collectives, per_device(): lax.all_to_all(summed, 'seq', split_axis=0, concat_axis=0, tiled=True)  23.2 us
    unnamed x19, local copies, waits for them, and re-layouts  13.8 us
    dot_general x1, matrix products, per_device(): jnp.dot(attn.reshape(-1, q_local * HD), w_out, preferred_element_type=jnp...  6.94 us
    dot_general x1, matrix products, per_device(): jnp.dot(flat, w_query, preferred_element_type=jnp.float32)  6.17 us
    dot_general x2, local copies, waits for them, and re-layouts, per_device(): keys = jnp.dot(flat, w_keyval[0], preferred_element_type=jnp.float32)  4.78 us
  transfers between devices with their start and end apart: 3, of which 3 were waited for; matrix products, arithmetic and copies ran while one was open for 13% of the time, Pallas kernels for 0%

profile of v1, /device:TPU:0, one launch (start us, length us, event | category | flops | bytes accessed | tf_op | source)
XLA Modules:
  0.0 173.1 jit_solution(15870984098198406333)
XLA Ops:
  6.5 1.9 %copy.33 = bf16[2,1,256,256]{2,3,1,0:T(8,128)(2,1)} copy(bf16[2,1,256,256]{3,2,1,0:T(8,128)(2,1)} %param.12) | data formatting | bytes 524288 | tf_op args[4]
  8.5 0.7 fusion.26
  9.8 0.6 gather_fusion.1
  10.4 1.0 broadcast_select_fusion
  11.5 0.6 dynamic_slice.11
  13.3 10.6 %copy.35 = bf16[5120,768]{0,1:T(8,128)(2,1)} copy(bf16[5120,768]{1,0:T(8,128)(2,1)} %param.13) | data formatting | bytes 15728640 | tf_op args[5]
  23.9 1.9 %slice_bitcast_fusion = bf16[256,5120]{0,1:T(8,128)(2,1)S(1)} fusion(bf16[2,5120,256]{2,1,0:T(8,128)(2,1)} %param.14), kind=kLoop, calls=%fused_computation.10 | loop fusion | bytes 5242880 | tf_op jit(solution)/shard_map/dot_general | solution.py:100
  25.9 2.9 %copy.39 = bf16[256,5120]{1,0:T(8,128)(2,1)} copy(bf16[256,5120]{0,1:T(8,128)(2,1)S(1)} %slice_bitcast_fusion) | data formatting | bytes 5242880 | tf_op jit(solution)/shard_map/dot_general | solution.py:100
  29.7 0.7 gather_fusion
  30.6 31.0 %all-gather.3.cloned.1.call-done = bf16[2,8,256,256]{2,3,1,0:T(8,128)(2,1)} async-done(((bf16[2,1,256,256]{2,3,1,0:T(8,128)(2,1)}), bf16[2,8,256,256]{2,3,1,0:T(8,128)(2,1)}) %all-gather.3.cloned.1.call-update) | async-done | bytes 2097168 | tf_op jit(solution)/shard_map/all_gather | solution.py:83
  61.6 1.6 constant_dynamic-slice_fusion.1
  63.3 24.0 %all-gather.5.cloned.1.call-done = bf16[16,16,5120]{2,1,0:T(8,128)(2,1)} async-done(((bf16[16,16,1280]{2,1,0:T(8,128)(2,1)}), bf16[16,16,5120]{2,1,0:T(8,128)(2,1)}) %all-gather.5.cloned.1.call-update) | async-done | bytes 2621456 | tf_op jit(solution)/shard_map/all_gather | solution.py:85
  87.3 6.2 %fusion.4 = f32[16,16,6,128]{3,1,2,0:T(8,128)S(1)} fusion(bf16[6,128,5120,1]{2,1,0,3:T(8,128)(2,1)} %bitcast.82, bf16[16,16,5120]{2,1,0:T(8,128)(2,1)} %all-gather.5.cloned.1.call-done), kind=kOutput, calls=%fused_computation.7 | convolution fusion | flops 2013265920 | bytes 11272192 | tf_op jit(solution)/shard_map/dot_general | solution.py:92
  93.9 0.9 fusion.2
  94.9 0.5 bitcast_reduce_fusion
  95.4 1.0 fusion.30
  96.8 0.6 fusion.8
  97.4 0.9 fusion.14
  98.7 0.5 copy-done.3
  99.2 0.8 fusion.13
  100.7 6.9 %convolution_convert_fusion = bf16[256,5120]{1,0:T(8,128)(2,1)} fusion(bf16[256,768]{1,0:T(8,128)(2,1)S(1)} %reshape_reshape.3, bf16[768,5120]{1,0:T(8,128)(2,1)} %param.15), kind=kOutput, calls=%fused_computation.2 | convolution fusion | flops 2014576640 | bytes 10878976 | tf_op jit(solution)/shard_map/dot_general | solution.py:108
  107.7 34.8 %reduce-scatter.2.cloned.1.call-done = bf16[16,16,1280]{2,1,0:T(8,128)(2,1)} async-done(((bf16[16,16,5120]{2,1,0:T(8,128)(2,1)}), bf16[16,16,1280]{2,1,0:T(8,128)(2,1)}) %reduce-scatter.2.cloned.1.call-update) | async-done | bytes 655376 | tf_op jit(solution)/shard_map/reduce_scatter | solution.py:111
  142.5 23.2 %all_to_all.5 = bf16[16,16,1280]{2,1,0:T(8,128)(2,1)S(1)} all-to-all(bf16[16,16,1280]{2,1,0:T(8,128)(2,1)} %reduce-scatter.2.cloned.1.call-done), channel_id=1, replica_groups=mesh['seq'=8,'tp'=4] {'seq'}, dimensions={0} | all-to-all | bytes 1310720 | tf_op jit(solution)/shard_map/all_to_all | solution.py:114
  165.7 0.8 copy.81
  (50 shorter events, 3.2 us)
Async XLA Ops:
  6.5 3.3 %copy-start = (bf16[16,16,1280]{2,1,0:T(8,128)(2,1)S(1)}, bf16[16,16,1280]{2,1,0:T(8,128)(2,1)}, u32[]{:S(2)}) copy-start(bf16[16,16,1280]{2,1,0:T(8,128)(2,1)} %param.8) | copy-start | bytes 1966084
  6.5 4.9 %copy-start.5 = (s32[8]{0:T(128)S(1)}, s32[8]{0:T(128)}, u32[]{:S(2)}) copy-start(s32[8]{0:T(128)} %param.11) | copy-start | bytes 100
  6.5 55.1 %all-gather.3.cloned.1.call-start = ((), (), s32[]{:S(2)}) async-start(), calls=%async_computation.2 | async-start | bytes 2359296 | tf_op jit(solution)/shard_map/all_gather | solution.py:83
  8.4 78.9 %all-gather.5.cloned.1.call-start = ((), (), s32[]{:S(2)}) async-start(), calls=%async_computation.3 | async-start | bytes 3276800 | tf_op jit(solution)/shard_map/all_gather | solution.py:85
  11.4 131.1 %reduce-scatter.2.cloned.1.call-start = ((), (), s32[]{:S(2)}) async-start(), calls=%async_computation.4 | async-start | bytes 3276800 | tf_op jit(solution)/shard_map/reduce_scatter | solution.py:111
  25.9 3.9 %copy-start.1 = (s32[128]{0:T(128)S(1)}, s32[128]{0:T(128)}, u32[]{:S(2)}) copy-start(s32[128]{0:T(128)} %param.9) | copy-start | bytes 1540
  87.3 6.5 %copy-start.2 = (bf16[256,5120]{1,0:T(8,128)(2,1)S(1)}, bf16[256,5120]{1,0:T(8,128)(2,1)}, u32[]{:S(2)}) copy-start(bf16[256,5120]{1,0:T(8,128)(2,1)} %copy.39) | copy-start | bytes 7864324
  87.3 6.5 %copy-start.4 = (bf16[16,16,5120]{2,1,0:T(8,128)(2,1)S(1)}, bf16[16,16,5120]{2,1,0:T(8,128)(2,1)}, u32[]{:S(2)}) copy-start(bf16[16,16,5120]{2,1,0:T(8,128)(2,1)} %all-gather.5.cloned.1.call-done) | copy-start | bytes 7864324
  93.5 3.8 %slice-start = ((s8[5242880]{0:T(1024)(128)(4,1)}), s8[4194304]{0:T(1024)(128)(4,1)S(1)}, s32[]{:S(2)}) async-start(s8[5242880]{0:T(1024)(128)(4,1)} %bitcast.89), calls=%async_computation.5 | async-start | bytes 8388608
  93.8 3.5 %slice-start.1 = ((s8[5242880]{0:T(1024)(128)(4,1)}), s8[1048576]{0:T(1024)(128)(4,1)S(1)}, s32[]{:S(2)}) async-start(s8[5242880]{0:T(1024)(128)(4,1)} %bitcast.89), calls=%async_computation.6 | async-start | bytes 2097152
  98.3 0.9 copy-start.3
Sparse Core Ops, SparseCore 0:
  9.5 52.0 all-gather.2
  63.2 24.0 all-gather.4
  107.8 34.6 reduce-scatter.1

commit v2 on v1

--- a/solution.py
+++ b/solution.py
@@ -2,11 +2,15 @@
 
 import jax
 import jax.numpy as jnp
+import numpy as np
 from jax import lax
+from jax.experimental import pallas as pl
+from jax.experimental.pallas import tpu as pltpu
 from jax.sharding import PartitionSpec as P
 
 HD = 128
 PL = 256
+RMAX = 16
 
 
 ROPE_BASE = 1000000.0
@@ -114,9 +118,384 @@
     return lax.all_to_all(summed, "seq", split_axis=0, concat_axis=0, tiled=True)
 
 
+MESH = pl.DeviceIdType.MESH
+ORDER = (6, 7, 4, 5, 2, 3, 1, 0)
+PIECES = 4
+
+
+def fused_kernel(
+    shard_ref, len_ref, prompt_ref, cos_ref, sin_ref, x_ref, kv_ref, wq_hbm, wkv_hbm, wo_hbm,
+    out_ref,
+    wq, wkv, wo, rows, acc, kbuf, vbuf, stage, landed, attn, queue, sibling, ahead, kept, across,
+    done, arrived,
+    load_sem, gather_send, gather_recv, line_send, line_recv, pair_send, pair_recv,
+    sib_send, sib_recv, cross_send, cross_recv, out_send, out_recv,
+):
+    seq = lax.axis_index("seq")
+    tp = lax.axis_index("tp")
+    z, x = seq // 2, seq % 2
+    y, c = tp // 2, tp % 2
+    sib = y * 2 + (1 - c)
+    opp = (1 - y) * 2 + c
+    diag = (1 - y) * 2 + (1 - c)
+    count, width = x_ref.shape
+    f32, bf16 = jnp.float32, jnp.bfloat16
+
+    def peer(m):
+        zz = (z, z + 1 - 2 * (z % 2), z + 2 - 4 * (z // 2), 3 - z)[m // 2]
+        return zz * 2 + (x, 1 - x)[m % 2]
+
+    loads = [
+        pltpu.make_async_copy(wq_hbm, wq, load_sem.at[0]),
+        pltpu.make_async_copy(wkv_hbm, wkv, load_sem.at[1]),
+        pltpu.make_async_copy(wo_hbm, wo, load_sem.at[2]),
+    ]
+    for load in loads:
+        load.start()
+
+    barrier = pltpu.get_barrier_semaphore()
+    for m in range(1, 8):
+        pl.semaphore_signal(barrier, inc=1, device_id=(peer(m), tp), device_id_type=MESH)
+    for other in (sib, opp):
+        pl.semaphore_signal(barrier, inc=1, device_id=(seq, other), device_id_type=MESH)
+    pl.semaphore_wait(barrier, 9)
+
+    def remote(src, dst, send, recv, device):
+        return pltpu.make_async_remote_copy(
+            src_ref=src, dst_ref=dst, send_sem=send, recv_sem=recv,
+            device_id=device, device_id_type=MESH,
+        )
+
+    size = count // PIECES
+    to_sib = remote(x_ref, rows.at[tp], gather_send.at[0], gather_recv.at[0], (seq, sib))
+    to_opp, forward = [], []
+    for i in range(PIECES):
+        part = pl.ds(i * size, size)
+        to_opp.append(
+            remote(
+                x_ref.at[part], rows.at[tp, part],
+                gather_send.at[1 + i], gather_recv.at[1 + i], (seq, opp),
+            )
+        )
+        forward.append(
+            remote(
+                rows.at[opp, part], rows.at[opp, part],
+                gather_send.at[1 + PIECES + i], gather_recv.at[1 + PIECES + i], (seq, sib),
+            )
+        )
+
+    bufs = (kbuf, vbuf)
+
+    def hop(kind, way, step):
+        block = z - step if way == 0 else z + step
+        target = (z + 1 if way == 0 else z - 1) * 2 + x
+        return remote(
+            bufs[kind].at[block], bufs[kind].at[block],
+            line_send.at[kind, way, step], line_recv.at[kind, block], (target, tp),
+        )
+
+    def can_send(way, step):
+        return (z < 3) & (z >= step) if way == 0 else (z > 0) & (z + step <= 3)
+
+    def has_source(way, step):
+        return z >= step if way == 0 else z + step <= 3
+
+    def launch(kind, step):
+        for way in (0, 1):
+            @pl.when(can_send(way, step))
+            def _():
+                hop(kind, way, step).start()
+
+    def receive(kind, step):
+        for way in (0, 1):
+            @pl.when(has_source(way, step))
+            def _():
+                block = z - step if way == 0 else z + step
+                remote(
+                    bufs[kind].at[block], bufs[kind].at[block],
+                    line_send.at[kind, way, 0], line_recv.at[kind, block], (seq, sib),
+                ).wait_recv()
+
+    kbuf[z] = kv_ref[0]
+    vbuf[z] = kv_ref[1]
+    for copy in to_opp:
+        copy.start()
+    launch(0, 0)
+    launch(1, 0)
+    to_sib.start()
+
+    def advance(step):
+        for kind in (0, 1):
+            receive(kind, step)
+            launch(kind, step)
+
+    def relay(i):
+        to_opp[i].wait_recv()
+        forward[i].start()
+
+    def project(owner, first):
+        base = pl.multiple_of(owner * width, width)
+
+        def add(n, value):
+            if first:
+                acc[n] = value
+            else:
+                acc[n] += value
+
+        source = x_ref if first else rows.at[owner]
+
+        def queries(n, carry):
+            lanes = pl.ds(pl.multiple_of(n * 256, 256), 256)
+            add(n, jnp.dot(source[...], wq[pl.ds(base, width), lanes], preferred_element_type=f32))
+            return carry
+
+        def keyval(n, carry):
+            add(3 + n, jnp.dot(source[...], wkv[n, pl.ds(base, width), :], preferred_element_type=f32))
+            return carry
+
+        lax.fori_loop(0, 3, queries, 0)
+        lax.fori_loop(0, 2, keyval, 0)
+
+    advance(1)
+    for i in range(PIECES // 2):
+        relay(i)
+    loads[0].wait()
+    loads[1].wait()
+    project(tp, True)
+    to_sib.wait_recv()
+    project(sib, False)
+    advance(2)
+    for i in range(PIECES // 2, PIECES - 1):
+        relay(i)
+
+    partner = peer(1)
+    wanted = prompt_ref[partner]
+    mine = prompt_ref[seq]
+
+    def pair(kind):
+        return remote(
+            stage.at[kind], landed.at[kind], pair_send.at[kind], pair_recv.at[kind], (partner, tp)
+        )
+
+    receive(0, 3)
+    stage[0] = kbuf[lax.shift_right_logical(wanted, 1)]
+    pair(0).start()
+    relay(PIECES - 1)
+    project(opp, False)
+    receive(1, 3)
+    stage[1] = vbuf[lax.shift_right_logical(wanted, 1)]
+    pair(1).start()
+    for i in range(PIECES):
+        forward[i].wait_recv()
+    project(diag, False)
+
+    lane = lax.broadcasted_iota(jnp.int32, (1, count), 1)
+    token = lax.rem(lane, RMAX)
+    owner_of = lax.div(lane, RMAX)
+    group = count // RMAX
+    shards = [shard_ref[seq * group + r] for r in range(group)]
+    place = jnp.full((1, count), -1, jnp.int32)
+    for r in range(group):
+        rank = jnp.int32(0)
+        for e in range(r):
+            rank = rank + jnp.where(shards[e] == shards[r], 1, 0)
+        slot = shards[r] * 2 + rank
+        here = (owner_of == r) & (token < len_ref[seq * group + r])
+        place = jnp.where(here, slot * RMAX + token, place)
+    down = lax.broadcasted_iota(jnp.int32, (count, count), 0)
+    across_i = lax.broadcasted_iota(jnp.int32, (count, count), 1)
+    deal = jnp.where(down == place, 1.0, 0.0).astype(bf16)
+    causal = (lax.div(down, RMAX) == lax.div(across_i, RMAX)) & (down >= across_i)
+
+    cosine = cos_ref[...]
+    sine = sin_ref[...]
+
+    def turn(values):
+        other = pltpu.roll(values, HD // 2, 1)
+        shape = (count // RMAX, RMAX, HD)
+        out = values.reshape(shape) * cosine[None] + other.reshape(shape) * sine[None]
+        return out.reshape(count, HD).astype(bf16)
+
+    local = lax.rem(mine, 2) == x
+    scale = 1.0 / math.sqrt(HD)
+    nt = (((1,), (1,)), ((), ()))
+    pair(0).wait_recv()
+    keys = jnp.where(local, kbuf[lax.shift_right_logical(mine, 1)], landed[0])
+    pair(1).wait_recv()
+    cached = jnp.where(local, vbuf[lax.shift_right_logical(mine, 1)], landed[1])
+    for h in range(6):
+        k = h // 3
+        lanes = slice(k * HD, (k + 1) * HD)
+        query = turn(acc[h // 2, :, (h % 2) * HD:(h % 2 + 1) * HD])
+        if h % 3 == 0:
+            own_key = turn(acc[3, :, lanes])
+            own_value = acc[4, :, lanes].astype(bf16)
+        prior = lax.dot_general(query, keys[:, lanes], nt, preferred_element_type=f32) * scale
+        recent = lax.dot_general(query, own_key, nt, preferred_element_type=f32) * scale
+        recent = jnp.where(causal, recent, -1e30)
+        top = jnp.maximum(
+            jnp.max(prior, -1, keepdims=True), jnp.max(recent, -1, keepdims=True)
+        )
+        prior = jnp.exp(prior - top)
+        recent = jnp.exp(recent - top)
+        share = 1.0 / (jnp.sum(prior, -1, keepdims=True) + jnp.sum(recent, -1, keepdims=True))
+        mixed = jnp.dot(
+            (prior * share).astype(bf16), cached[:, lanes], preferred_element_type=f32
+        ) + jnp.dot((recent * share).astype(bf16), own_value, preferred_element_type=f32)
+        mixed = jnp.dot(deal, mixed.astype(bf16), preferred_element_type=f32)
+        attn[:, h * HD:(h + 1) * HD] = mixed.astype(bf16)
+
+    loads[2].wait()
+
+    def partial(owner, dst):
+        def tile(n, carry):
+            source = pl.ds(pl.multiple_of(owner * width + n * 256, 256), 256)
+            lanes = pl.ds(pl.multiple_of(n * 256, 256), 256)
+            dst[:, lanes] = jnp.dot(
+                attn[...], wo[:, source], preferred_element_type=f32
+            ).astype(bf16)
+            return carry
+
+        lax.fori_loop(0, width // 256, tile, 0)
+
+    def swap(i):
+        return remote(queue.at[i], sibling.at[i], sib_send.at[i], sib_recv.at[i], (seq, sib))
+
+    span = count // 8
+
+    def chunk(m):
+        return pl.ds(pl.multiple_of(peer(m) * span, span), span)
+
+    def cross(m):
+        return remote(
+            ahead.at[chunk(m)], across.at[chunk(m)], cross_send.at[m], cross_recv.at[m], (seq, opp)
+        )
+
+    def deliver(m):
+        return remote(
+            done.at[chunk(m)], arrived.at[seq], out_send.at[m], out_recv.at[m], (peer(m), tp)
+        )
+
+    def accept(m):
+        return remote(
+            done.at[chunk(m)], arrived.at[peer(m)], out_send.at[m], out_recv.at[m], (peer(m), tp)
+        )
+
+    partial(diag, queue.at[0])
+    swap(0).start()
+    partial(opp, ahead)
+    swap(0).wait_recv()
+    for m in ORDER:
+        both = ahead[chunk(m)].astype(f32) + sibling[0, chunk(m)].astype(f32)
+        ahead[chunk(m)] = both.astype(bf16)
+        cross(m).start()
+    partial(sib, queue.at[1])
+    swap(1).start()
+    partial(tp, kept)
+    swap(1).wait_recv()
+    for m in ORDER:
+        cross(m).wait_recv()
+        total = kept[chunk(m)].astype(f32) + sibling[1, chunk(m)].astype(f32)
+        total = (total + across[chunk(m)].astype(f32)).astype(bf16)
+        if m == 0:
+            out_ref[chunk(0)] = total
+        else:
+            done[chunk(m)] = total
+            deliver(m).start()
+    for m in ORDER[:-1]:
+        accept(m).wait_recv()
+        out_ref[chunk(m)] = arrived[peer(m)]
+
+    to_sib.wait_send()
+    for i in range(PIECES):
+        to_opp[i].wait_send()
+        forward[i].wait_send()
+    for kind in (0, 1):
+        for step in range(3):
+            for way in (0, 1):
+                @pl.when(can_send(way, step))
+                def _():
+                    hop(kind, way, step).wait_send()
+        pair(kind).wait_send()
+        swap(kind).wait_send()
+    for m in range(8):
+        cross(m).wait_send()
+    for m in range(1, 8):
+        deliver(m).wait_send()
+
+
+def fused_device(resp_rows, resp_len, resp_shard, group_prompt, prompt_kv, w_query, w_keyval, w_out):
+    group, tokens, width = resp_rows.shape
+    count = group * tokens
+    angles = np.arange(PL, PL + tokens, dtype=np.float32)[:, None] * (
+        ROPE_BASE ** (-np.arange(0, HD, 2, dtype=np.float64) / HD)
+    ).astype(np.float32)
+    cosine = np.concatenate([np.cos(angles), np.cos(angles)], -1).astype(np.float32)
+    sine = np.concatenate([-np.sin(angles), np.sin(angles)], -1).astype(np.float32)
+    bf16 = jnp.bfloat16
+    block = (count, width)
+    smem = pl.BlockSpec(memory_space=pltpu.SMEM)
+    vmem = pl.BlockSpec(memory_space=pltpu.VMEM)
+    hbm = pl.BlockSpec(memory_space=pl.ANY)
+    dma = pltpu.SemaphoreType.DMA
+    cache = (PL, w_keyval.shape[2])
+    out = pl.pallas_call(
+        fused_kernel,
+        out_shape=jax.ShapeDtypeStruct(block, bf16),
+        in_specs=[smem] * 3 + [vmem] * 4 + [hbm] * 3,
+        out_specs=vmem,
+        scratch_shapes=[
+            pltpu.VMEM(w_query.shape, bf16),
+            pltpu.VMEM(w_keyval.shape, bf16),
+            pltpu.VMEM(w_out.shape, bf16),
+            pltpu.VMEM((4,) + block, bf16),
+            pltpu.VMEM((5, count, 256), jnp.float32),
+            pltpu.VMEM((4,) + cache, bf16),
+            pltpu.VMEM((4,) + cache, bf16),
+            pltpu.VMEM((2,) + cache, bf16),
+            pltpu.VMEM((2,) + cache, bf16),
+            pltpu.VMEM((count, w_query.shape[1]), bf16),
+            pltpu.VMEM((2,) + block, bf16),
+            pltpu.VMEM((2,) + block, bf16),
+            pltpu.VMEM(block, bf16),
+            pltpu.VMEM(block, bf16),
+            pltpu.VMEM(block, bf16),
+            pltpu.VMEM(block, bf16),
+            pltpu.VMEM((8, count // 8, width), bf16),
+            dma((3,)),
+            dma((1 + 2 * PIECES,)),
+            dma((1 + 2 * PIECES,)),
+            dma((2, 2, 3)),
+            dma((2, 4)),
+            dma((2,)),
+            dma((2,)),
+            dma((2,)),
+            dma((2,)),
+            dma((8,)),
+            dma((8,)),
+            dma((8,)),
+            dma((8,)),
+        ],
+        compiler_params=pltpu.CompilerParams(
+            collective_id=0, has_side_effects=True, vmem_limit_bytes=56 * 1024 * 1024
+        ),
+        cost_estimate=pl.CostEstimate(
+            flops=6 * 10**9, bytes_accessed=23 * 10**6, transcendentals=10**6
+        ),
+    )(
+        resp_shard[:, 0], resp_len, group_prompt, jnp.asarray(cosine), jnp.asarray(sine),
+        resp_rows.reshape(block), prompt_kv[:, 0], w_query, w_keyval, w_out,
+    )
+    return out.reshape(group, tokens, width)
+
+
+def fits(mesh):
+    return mesh.shape["seq"] == 8 and mesh.shape["tp"] == 4
+
+
 def solution(mesh):
     return jax.shard_map(
-        per_device,
+        fused_device if fits(mesh) else per_device,
         mesh=mesh,
         in_specs=(
             P("seq", None, "tp"),

time: 174 us -> 60.5 us (0.35)
  waiting for transfers between devices: 89.9 us -> 0 us
  Pallas kernels: 0 us -> 58.3 us
  blocking collectives: 23.2 us -> 0 us
  local copies, waits for them, and re-layouts: 24 us -> 1.97 us
  matrix products: 17.6 us -> 0 us
  between operations: 15.2 us -> 0.01 us
  other arithmetic: 3.01 us -> 0 us
    pallas_call x0 -> x1, Pallas kernels: none -> 58.3 us  [fused_device(): pl.pallas_call(fused_kernel, out_shape=jax.ShapeDtypeStruct(block, bf16),...]
    all_gather x2 -> x0, waiting for transfers between devices: 55 us -> none  [the longest x1 31 us: per_device(): caches = lax.all_gather(prompt_kv, 'seq', axis=1, tiled=True)]
    reduce_scatter x1 -> x0, waiting for transfers between devices: 34.8 us -> none  [per_device(): lax.psum_scatter(partial_value.reshape(slots, token_count, -1), 'tp', sca...]
    all_to_all x1 -> x0, blocking collectives: 23.2 us -> none  [per_device(): lax.all_to_all(summed, 'seq', split_axis=0, concat_axis=0, tiled=True)]
    dot_general x8 -> x0, matrix products: 17.6 us -> none  [the longest x1 6.94 us: per_device(): jnp.dot(attn.reshape(-1, q_local * HD), w_out, preferred_element_type=jnp...]
    unnamed x19 -> x1, local copies, waits for them, and re-layouts: 13.8 us -> 1.97 us
    dot_general x2 -> x0, local copies, waits for them, and re-layouts: 4.78 us -> none  [per_device(): keys = jnp.dot(flat, w_keyval[0], preferred_element_type=jnp.float32)]
  transfers between devices with their start and end apart: 3 -> 0, of which waited for: 3 -> 0; matrix products, arithmetic and copies ran while one was open for 13% -> 0% of each run, Pallas kernels for 0% -> 0%
where the time goes in v2:
time: 60.5 us; the launch traced here: 60.3 us
  Pallas kernels  58.3 us (96%)
  local copies, waits for them, and re-layouts  1.97 us (3%)
    pallas_call x1, Pallas kernels, fused_device(): pl.pallas_call(fused_kernel, out_shape=jax.ShapeDtypeStruct(block, bf16),...  58.3 us
    unnamed x1, local copies, waits for them, and re-layouts  1.97 us

profile of v2, /device:TPU:0, one launch (start us, length us, event | category | flops | bytes accessed | tf_op | source)
XLA Modules:
  0.0 60.3 jit_solution(10908891373457413821)
XLA Ops:
  0.0 58.3 %shard_map.100 = bf16[256,1280]{1,0:T(8,128)(2,1)} custom-call(s32[128]{0:T(128)} %bitcast.7, s32[128]{0:T(128)} %len_ref.1, s32[8]{0:T(128)} %prompt_ref.1, f32[16,128]{1,0:T(8,128)} %constant.4.clone.cos_ref, f32[16,128]{1,0:T(8,128)} %constant.5.clone.sin_ref, bf16[256,1280]{1,0:T(8,128)(2,1)} %bitcast.5, bf16[2,256,256]{2,1,0:T(8,128)(2,1)} %bitcast.6, ...), custom_call_target="tpu_custom_call" | custom-call | flops 6000000000 | bytes 23000000 | tf_op jit(solution)/shard_map/pallas_call | solution.py:442
  58.3 2.0 %copy.12 = bf16[16,16,1280]{2,1,0:T(8,128)(2,1)} copy(bf16[16,16,1280]{2,1,0:T(8,128)(2,1)} %bitcast.4) | data formatting | bytes 1310720

commit v3 on v2

--- a/solution.py
+++ b/solution.py
@@ -124,10 +124,10 @@
 
 
 def fused_kernel(
-    shard_ref, len_ref, prompt_ref, cos_ref, sin_ref, x_ref, kv_ref, wq_hbm, wkv_hbm, wo_hbm,
+    shard_ref, len_ref, prompt_ref, cos_hbm, sin_hbm, x_hbm, kv_hbm, wq_hbm, wkv_hbm, wo_hbm,
     out_ref,
-    wq, wkv, wo, rows, acc, kbuf, vbuf, stage, landed, attn, queue, sibling, ahead, kept, across,
-    done, arrived,
+    wq, wkv, wo, rows, acc, cos_ref, sin_ref, buf0, buf1, buf2, buf3, stage, landed, dealt, valid,
+    attn, queue, sibling, ahead, kept, across, done,
     load_sem, gather_send, gather_recv, line_send, line_recv, pair_send, pair_recv,
     sib_send, sib_recv, cross_send, cross_recv, out_send, out_recv,
 ):
@@ -138,19 +138,26 @@
     sib = y * 2 + (1 - c)
     opp = (1 - y) * 2 + c
     diag = (1 - y) * 2 + (1 - c)
-    count, width = x_ref.shape
+    count, width = x_hbm.shape
     f32, bf16 = jnp.float32, jnp.bfloat16
+    bufs = (buf0, buf1, buf2, buf3)
+    part_len = PL // 2
 
     def peer(m):
         zz = (z, z + 1 - 2 * (z % 2), z + 2 - 4 * (z // 2), 3 - z)[m // 2]
         return zz * 2 + (x, 1 - x)[m % 2]
 
-    loads = [
-        pltpu.make_async_copy(wq_hbm, wq, load_sem.at[0]),
-        pltpu.make_async_copy(wkv_hbm, wkv, load_sem.at[1]),
-        pltpu.make_async_copy(wo_hbm, wo, load_sem.at[2]),
+    def local(src, dst, i):
+        return pltpu.make_async_copy(src, dst, load_sem.at[i])
+
+    x_load = local(x_hbm, rows.at[tp], 0)
+    kv_loads = [
+        local(kv_hbm.at[k // 2, pl.ds((k % 2) * part_len, part_len)], bufs[k].at[z], 1 + k)
+        for k in range(4)
     ]
-    for load in loads:
+    tables = [local(cos_hbm, cos_ref, 5), local(sin_hbm, sin_ref, 6)]
+    loads = [local(wq_hbm, wq, 7), local(wkv_hbm, wkv, 8), local(wo_hbm, wo, 9)]
+    for load in [x_load] + kv_loads + tables + loads:
         load.start()
 
     barrier = pltpu.get_barrier_semaphore()
@@ -167,13 +174,13 @@
         )
 
     size = count // PIECES
-    to_sib = remote(x_ref, rows.at[tp], gather_send.at[0], gather_recv.at[0], (seq, sib))
+    to_sib = remote(rows.at[tp], rows.at[tp], gather_send.at[0], gather_recv.at[0], (seq, sib))
     to_opp, forward = [], []
     for i in range(PIECES):
         part = pl.ds(i * size, size)
         to_opp.append(
             remote(
-                x_ref.at[part], rows.at[tp, part],
+                rows.at[tp, part], rows.at[tp, part],
                 gather_send.at[1 + i], gather_recv.at[1 + i], (seq, opp),
             )
         )
@@ -183,8 +190,6 @@
                 gather_send.at[1 + PIECES + i], gather_recv.at[1 + PIECES + i], (seq, sib),
             )
         )
-
-    bufs = (kbuf, vbuf)
 
     def hop(kind, way, step):
         block = z - step if way == 0 else z + step
@@ -216,16 +221,16 @@
                     line_send.at[kind, way, 0], line_recv.at[kind, block], (seq, sib),
                 ).wait_recv()
 
-    kbuf[z] = kv_ref[0]
-    vbuf[z] = kv_ref[1]
+    x_load.wait()
     for copy in to_opp:
         copy.start()
-    launch(0, 0)
-    launch(1, 0)
+    for kind in range(4):
+        kv_loads[kind].wait()
+        launch(kind, 0)
     to_sib.start()
 
-    def advance(step):
-        for kind in (0, 1):
+    def advance(step, kinds):
+        for kind in kinds:
             receive(kind, step)
             launch(kind, step)
 
@@ -242,7 +247,7 @@
             else:
                 acc[n] += value
 
-        source = x_ref if first else rows.at[owner]
+        source = rows.at[owner]
 
         def queries(n, carry):
             lanes = pl.ds(pl.multiple_of(n * 256, 256), 256)
@@ -256,38 +261,32 @@
         lax.fori_loop(0, 3, queries, 0)
         lax.fori_loop(0, 2, keyval, 0)
 
-    advance(1)
-    for i in range(PIECES // 2):
-        relay(i)
+    partner = peer(1)
+    wanted = lax.shift_right_logical(prompt_ref[partner], 1)
+
+    def pair(kind):
+        return remote(
+            stage.at[kind], landed.at[kind], pair_send.at[kind], pair_recv.at[kind], (partner, tp)
+        )
+
+    def hand_over(kind):
+        receive(kind, 3)
+        stage[kind] = bufs[kind][wanted]
+        pair(kind).start()
+
+    advance(1, (0, 1, 2, 3))
     loads[0].wait()
     loads[1].wait()
     project(tp, True)
+    relay(0)
+    advance(2, (0, 1))
+    relay(1)
     to_sib.wait_recv()
     project(sib, False)
-    advance(2)
-    for i in range(PIECES // 2, PIECES - 1):
-        relay(i)
-
-    partner = peer(1)
-    wanted = prompt_ref[partner]
-    mine = prompt_ref[seq]
-
-    def pair(kind):
-        return remote(
-            stage.at[kind], landed.at[kind], pair_send.at[kind], pair_recv.at[kind], (partner, tp)
-        )
-
-    receive(0, 3)
-    stage[0] = kbuf[lax.shift_right_logical(wanted, 1)]
-    pair(0).start()
-    relay(PIECES - 1)
-    project(opp, False)
-    receive(1, 3)
-    stage[1] = vbuf[lax.shift_right_logical(wanted, 1)]
-    pair(1).start()
-    for i in range(PIECES):
-        forward[i].wait_recv()
-    project(diag, False)
+    advance(2, (2, 3))
+    relay(2)
+    hand_over(0)
+    hand_over(1)
 
     lane = lax.broadcasted_iota(jnp.int32, (1, count), 1)
     token = lax.rem(lane, RMAX)
@@ -303,10 +302,25 @@
         here = (owner_of == r) & (token < len_ref[seq * group + r])
         place = jnp.where(here, slot * RMAX + token, place)
     down = lax.broadcasted_iota(jnp.int32, (count, count), 0)
-    across_i = lax.broadcasted_iota(jnp.int32, (count, count), 1)
     deal = jnp.where(down == place, 1.0, 0.0).astype(bf16)
-    causal = (lax.div(down, RMAX) == lax.div(across_i, RMAX)) & (down >= across_i)
-
+    valid[...] = jnp.broadcast_to(
+        jnp.sum(deal.astype(f32), -1, keepdims=True), valid.shape
+    )
+    half = count // 2
+    row = lax.broadcasted_iota(jnp.int32, (half, half), 0)
+    col = lax.broadcasted_iota(jnp.int32, (half, half), 1)
+    causal = (lax.div(row, RMAX) == lax.div(col, RMAX)) & (row >= col)
+
+    relay(PIECES - 1)
+    project(opp, False)
+    hand_over(2)
+    hand_over(3)
+    for i in range(PIECES):
+        forward[i].wait_recv()
+    project(diag, False)
+
+    for table in tables:
+        table.wait()
     cosine = cos_ref[...]
     sine = sin_ref[...]
 
@@ -316,50 +330,73 @@
         out = values.reshape(shape) * cosine[None] + other.reshape(shape) * sine[None]
         return out.reshape(count, HD).astype(bf16)
 
-    local = lax.rem(mine, 2) == x
+    for n in range(5):
+        if n < 4:
+            tile = jnp.concatenate([turn(acc[n, :, :HD]), turn(acc[n, :, HD:])], -1)
+        else:
+            tile = acc[n].astype(bf16)
+        dealt[n] = jnp.dot(deal, tile, preferred_element_type=f32).astype(bf16)
+
+    mine = prompt_ref[seq]
+    here_too = lax.rem(mine, 2) == x
     scale = 1.0 / math.sqrt(HD)
     nt = (((1,), (1,)), ((), ()))
-    pair(0).wait_recv()
-    keys = jnp.where(local, kbuf[lax.shift_right_logical(mine, 1)], landed[0])
-    pair(1).wait_recv()
-    cached = jnp.where(local, vbuf[lax.shift_right_logical(mine, 1)], landed[1])
-    for h in range(6):
-        k = h // 3
-        lanes = slice(k * HD, (k + 1) * HD)
-        query = turn(acc[h // 2, :, (h % 2) * HD:(h % 2 + 1) * HD])
-        if h % 3 == 0:
-            own_key = turn(acc[3, :, lanes])
-            own_value = acc[4, :, lanes].astype(bf16)
-        prior = lax.dot_general(query, keys[:, lanes], nt, preferred_element_type=f32) * scale
-        recent = lax.dot_general(query, own_key, nt, preferred_element_type=f32) * scale
-        recent = jnp.where(causal, recent, -1e30)
-        top = jnp.maximum(
-            jnp.max(prior, -1, keepdims=True), jnp.max(recent, -1, keepdims=True)
-        )
-        prior = jnp.exp(prior - top)
-        recent = jnp.exp(recent - top)
-        share = 1.0 / (jnp.sum(prior, -1, keepdims=True) + jnp.sum(recent, -1, keepdims=True))
-        mixed = jnp.dot(
-            (prior * share).astype(bf16), cached[:, lanes], preferred_element_type=f32
-        ) + jnp.dot((recent * share).astype(bf16), own_value, preferred_element_type=f32)
-        mixed = jnp.dot(deal, mixed.astype(bf16), preferred_element_type=f32)
-        attn[:, h * HD:(h + 1) * HD] = mixed.astype(bf16)
-
-    loads[2].wait()
-
-    def partial(owner, dst):
+
+    def fetch(kind):
+        pair(kind).wait_recv()
+        return jnp.where(here_too, bufs[kind][lax.shift_right_logical(mine, 1)], landed[kind])
+
+    for kind in range(4):
+        landed[kind] = fetch(kind)
+
+    def attend_rows(base):
+        span_rows = pl.ds(base, half)
+        mask = valid[span_rows, :1]
+        for h in range(6):
+            k = h // 3
+            lanes = slice(k * HD, (k + 1) * HD)
+            query = dealt[h // 2, span_rows, (h % 2) * HD:(h % 2 + 1) * HD]
+            own_key = dealt[3, span_rows, lanes]
+            own_value = dealt[4, span_rows, lanes]
+            first = lax.dot_general(query, landed[0, :, lanes], nt, preferred_element_type=f32)
+            second = lax.dot_general(query, landed[1, :, lanes], nt, preferred_element_type=f32)
+            recent = lax.dot_general(query, own_key, nt, preferred_element_type=f32) * scale
+            first, second = first * scale, second * scale
+            recent = jnp.where(causal, recent, -1e30)
+            top = jnp.max(
+                jnp.maximum(jnp.maximum(first, second), recent), -1, keepdims=True
+            )
+            first, second = jnp.exp(first - top), jnp.exp(second - top)
+            recent = jnp.exp(recent - top)
+            share = mask / jnp.sum(first + second + recent, -1, keepdims=True)
+            mixed = (
+                jnp.dot((first * share).astype(bf16), landed[2, :, lanes],
+                        preferred_element_type=f32)
+                + jnp.dot((second * share).astype(bf16), landed[3, :, lanes],
+                          preferred_element_type=f32)
+                + jnp.dot((recent * share).astype(bf16), own_value, preferred_element_type=f32)
+            )
+            attn[span_rows, h * HD:(h + 1) * HD] = mixed.astype(bf16)
+
+    def partial(owner, dst, base):
+        span_rows = pl.ds(base, half)
+
         def tile(n, carry):
             source = pl.ds(pl.multiple_of(owner * width + n * 256, 256), 256)
             lanes = pl.ds(pl.multiple_of(n * 256, 256), 256)
-            dst[:, lanes] = jnp.dot(
-                attn[...], wo[:, source], preferred_element_type=f32
+            dst[span_rows, lanes] = jnp.dot(
+                attn[span_rows], wo[:, source], preferred_element_type=f32
             ).astype(bf16)
             return carry
 
         lax.fori_loop(0, width // 256, tile, 0)
 
-    def swap(i):
-        return remote(queue.at[i], sibling.at[i], sib_send.at[i], sib_recv.at[i], (seq, sib))
+    def swap(i, side):
+        span_rows = pl.ds(bases[side], half)
+        return remote(
+            queue.at[i, span_rows], sibling.at[i, span_rows],
+            sib_send.at[i, side], sib_recv.at[i, side], (seq, sib),
+        )
 
     span = count // 8
 
@@ -371,53 +408,85 @@
             ahead.at[chunk(m)], across.at[chunk(m)], cross_send.at[m], cross_recv.at[m], (seq, opp)
         )
 
+    home = pl.ds(pl.multiple_of(seq * span, span), span)
+
     def deliver(m):
         return remote(
-            done.at[chunk(m)], arrived.at[seq], out_send.at[m], out_recv.at[m], (peer(m), tp)
+            done.at[chunk(m)], out_ref.at[home], out_send.at[m], out_recv.at[m], (peer(m), tp)
         )
 
     def accept(m):
         return remote(
-            done.at[chunk(m)], arrived.at[peer(m)], out_send.at[m], out_recv.at[m], (peer(m), tp)
-        )
-
-    partial(diag, queue.at[0])
-    swap(0).start()
-    partial(opp, ahead)
-    swap(0).wait_recv()
-    for m in ORDER:
+            done.at[chunk(m)], out_ref.at[chunk(m)], out_send.at[m], out_recv.at[m], (peer(m), tp)
+        )
+
+    stay = pltpu.make_async_copy(done.at[home], out_ref.at[home], out_send.at[0])
+
+    def pass_on(m):
         both = ahead[chunk(m)].astype(f32) + sibling[0, chunk(m)].astype(f32)
         ahead[chunk(m)] = both.astype(bf16)
         cross(m).start()
-    partial(sib, queue.at[1])
-    swap(1).start()
-    partial(tp, kept)
-    swap(1).wait_recv()
-    for m in ORDER:
+
+    def finish(m):
         cross(m).wait_recv()
         total = kept[chunk(m)].astype(f32) + sibling[1, chunk(m)].astype(f32)
-        total = (total + across[chunk(m)].astype(f32)).astype(bf16)
+        done[chunk(m)] = (total + across[chunk(m)].astype(f32)).astype(bf16)
         if m == 0:
-            out_ref[chunk(0)] = total
+            stay.start()
         else:
-            done[chunk(m)] = total
             deliver(m).start()
+
+    bases = (
+        pl.multiple_of((1 - z // 2) * half, half),
+        pl.multiple_of((z // 2) * half, half),
+    )
+    loads[2].wait()
+    attend_rows(bases[0])
+    partial(diag, queue.at[0], bases[0])
+    swap(0, 0).start()
+    partial(opp, ahead, bases[0])
+    partial(sib, queue.at[1], bases[0])
+    swap(1, 0).start()
+    swap(0, 0).wait_recv()
+    for m in ORDER[:4]:
+        pass_on(m)
+    partial(tp, kept, bases[0])
+    attend_rows(bases[1])
+    swap(1, 0).wait_recv()
+    finish(ORDER[0])
+    partial(diag, queue.at[0], bases[1])
+    swap(0, 1).start()
+    partial(opp, ahead, bases[1])
+    partial(sib, queue.at[1], bases[1])
+    swap(1, 1).start()
+    swap(0, 1).wait_recv()
+    for m in ORDER[4:]:
+        pass_on(m)
+    finish(ORDER[1])
+    partial(tp, kept, bases[1])
+    finish(ORDER[2])
+    finish(ORDER[3])
+    swap(1, 1).wait_recv()
+    for m in ORDER[4:]:
+        finish(m)
     for m in ORDER[:-1]:
         accept(m).wait_recv()
-        out_ref[chunk(m)] = arrived[peer(m)]
+    stay.wait()
 
     to_sib.wait_send()
     for i in range(PIECES):
         to_opp[i].wait_send()
         forward[i].wait_send()
-    for kind in (0, 1):
+    for kind in range(4):
         for step in range(3):
             for way in (0, 1):
                 @pl.when(can_send(way, step))
                 def _():
                     hop(kind, way, step).wait_send()
         pair(kind).wait_send()
-        swap(kind).wait_send()
+    for i in (0, 1):
+        for side in (0, 1):
+            swap(i, side).wait_send()
     for m in range(8):
         cross(m).wait_send()
     for m in range(1, 8):
@@ -435,25 +504,30 @@
     bf16 = jnp.bfloat16
     block = (count, width)
     smem = pl.BlockSpec(memory_space=pltpu.SMEM)
-    vmem = pl.BlockSpec(memory_space=pltpu.VMEM)
     hbm = pl.BlockSpec(memory_space=pl.ANY)
     dma = pltpu.SemaphoreType.DMA
-    cache = (PL, w_keyval.shape[2])
+    cache = (PL // 2, w_keyval.shape[2])
     out = pl.pallas_call(
         fused_kernel,
         out_shape=jax.ShapeDtypeStruct(block, bf16),
-        in_specs=[smem] * 3 + [vmem] * 4 + [hbm] * 3,
-        out_specs=vmem,
+        in_specs=[smem] * 3 + [hbm] * 7,
+        out_specs=hbm,
         scratch_shapes=[
             pltpu.VMEM(w_query.shape, bf16),
             pltpu.VMEM(w_keyval.shape, bf16),
             pltpu.VMEM(w_out.shape, bf16),
             pltpu.VMEM((4,) + block, bf16),
             pltpu.VMEM((5, count, 256), jnp.float32),
+            pltpu.VMEM((tokens, HD), jnp.float32),
+            pltpu.VMEM((tokens, HD), jnp.float32),
             pltpu.VMEM((4,) + cache, bf16),
             pltpu.VMEM((4,) + cache, bf16),
-            pltpu.VMEM((2,) + cache, bf16),
-            pltpu.VMEM((2,) + cache, bf16),
+            pltpu.VMEM((4,) + cache, bf16),
+            pltpu.VMEM((4,) + cache, bf16),
+            pltpu.VMEM((4,) + cache, bf16),
+            pltpu.VMEM((4,) + cache, bf16),
+            pltpu.VMEM((5, count, 256), bf16),
+            pltpu.VMEM((count, HD), jnp.float32),
             pltpu.VMEM((count, w_query.shape[1]), bf16),
             pltpu.VMEM((2,) + block, bf16),
             pltpu.VMEM((2,) + block, bf16),
@@ -461,16 +535,15 @@
             pltpu.VMEM(block, bf16),
             pltpu.VMEM(block, bf16),
             pltpu.VMEM(block, bf16),
-            pltpu.VMEM((8, count // 8, width), bf16),
-            dma((3,)),
+            dma((10,)),
             dma((1 + 2 * PIECES,)),
             dma((1 + 2 * PIECES,)),
-            dma((2, 2, 3)),
-            dma((2, 4)),
-            dma((2,)),
-            dma((2,)),
-            dma((2,)),
-            dma((2,)),
+            dma((4, 2, 3)),
+            dma((4, 4)),
+            dma((4,)),
+            dma((4,)),
+            dma((2, 2)),
+            dma((2, 2)),
             dma((8,)),
             dma((8,)),
             dma((8,)),

time: 60.5 us -> 59 us (0.975)
  Pallas kernels: 58.3 us -> 56.9 us
    pallas_call x1, Pallas kernels: 58.3 us -> 56.9 us  [fused_device(): pl.pallas_call(fused_kernel, out_shape=jax.ShapeDtypeStruct(block, bf16),...]
where the time goes in v3:
time: 59 us; the launch traced here: 58.8 us
  Pallas kernels  56.9 us (96%)
  local copies, waits for them, and re-layouts  1.97 us (3%)
    pallas_call x1, Pallas kernels, fused_device(): pl.pallas_call(fused_kernel, out_shape=jax.ShapeDtypeStruct(block, bf16),...  56.9 us
    unnamed x1, local copies, waits for them, and re-layouts  1.97 us

profile of v3, /device:TPU:0, one launch (start us, length us, event | category | flops | bytes accessed | tf_op | source)
XLA Modules:
  0.0 58.8 jit_solution(9834173620904441079)
XLA Ops:
  0.0 56.9 %shard_map.100 = bf16[256,1280]{1,0:T(8,128)(2,1)} custom-call(s32[128]{0:T(128)} %bitcast.7, s32[128]{0:T(128)} %len_ref.1, s32[8]{0:T(128)} %prompt_ref.1, f32[16,128]{1,0:T(8,128)} %constant.4.clone.cos_hbm, f32[16,128]{1,0:T(8,128)} %constant.5.clone.sin_hbm, bf16[256,1280]{1,0:T(8,128)(2,1)} %bitcast.5, bf16[2,256,256]{2,1,0:T(8,128)(2,1)} %bitcast.6, ...), custom_call_target="tpu_custom_call" | custom-call | flops 6000000000 | bytes 23000000 | tf_op jit(solution)/shard_map/pallas_call | solution.py:510
  56.9 2.0 %copy.12 = bf16[16,16,1280]{2,1,0:T(8,128)(2,1)} copy(bf16[16,16,1280]{2,1,0:T(8,128)(2,1)} %bitcast.4) | data formatting | bytes 1310720

commit v4 on v3

--- a/solution.py
+++ b/solution.py
@@ -120,7 +120,7 @@
 
 MESH = pl.DeviceIdType.MESH
 ORDER = (6, 7, 4, 5, 2, 3, 1, 0)
-PIECES = 4
+PIECES = 5
 
 
 def fused_kernel(
@@ -156,9 +156,20 @@
         for k in range(4)
     ]
     tables = [local(cos_hbm, cos_ref, 5), local(sin_hbm, sin_ref, 6)]
-    loads = [local(wq_hbm, wq, 7), local(wkv_hbm, wkv, 8), local(wo_hbm, wo, 9)]
-    for load in [x_load] + kv_loads + tables + loads:
+    blocks = []
+    for i, owner in enumerate((tp, sib, opp, diag)):
+        part = pl.ds(pl.multiple_of(owner * width, width), width)
+        blocks.append((
+            local(wq_hbm.at[part], wq.at[part], 7 + 2 * i),
+            local(wkv_hbm.at[:, part], wkv.at[:, part], 8 + 2 * i),
+        ))
+    wo_load = local(wo_hbm, wo, 15)
+    for load in [x_load] + kv_loads + tables:
         load.start()
+    for block in blocks:
+        for load in block:
+            load.start()
+    wo_load.start()
 
     barrier = pltpu.get_barrier_semaphore()
     for m in range(1, 8):
@@ -173,20 +184,20 @@
             device_id=device, device_id_type=MESH,
         )
 
-    size = count // PIECES
+    size = width // PIECES
     to_sib = remote(rows.at[tp], rows.at[tp], gather_send.at[0], gather_recv.at[0], (seq, sib))
     to_opp, forward = [], []
     for i in range(PIECES):
         part = pl.ds(i * size, size)
         to_opp.append(
             remote(
-                rows.at[tp, part], rows.at[tp, part],
+                rows.at[tp, :, part], rows.at[tp, :, part],
                 gather_send.at[1 + i], gather_recv.at[1 + i], (seq, opp),
             )
         )
         forward.append(
             remote(
-                rows.at[opp, part], rows.at[opp, part],
+                rows.at[opp, :, part], rows.at[opp, :, part],
                 gather_send.at[1 + PIECES + i], gather_recv.at[1 + PIECES + i], (seq, sib),
             )
         )
@@ -238,55 +249,40 @@
         to_opp[i].wait_recv()
         forward[i].start()
 
-    def project(owner, first):
-        base = pl.multiple_of(owner * width, width)
-
-        def add(n, value):
+    def project(owner, start, depth, first):
+        base = pl.multiple_of(owner * width + start, 256)
+        source = rows[owner, :, start:start + depth]
+        for n in range(5):
+            if n < 3:
+                weight = wq[pl.ds(base, depth), n * 256:(n + 1) * 256]
+            else:
+                weight = wkv[n - 3, pl.ds(base, depth), :]
+            value = jnp.dot(source, weight, preferred_element_type=f32)
             if first:
                 acc[n] = value
             else:
                 acc[n] += value
 
-        source = rows.at[owner]
-
-        def queries(n, carry):
-            lanes = pl.ds(pl.multiple_of(n * 256, 256), 256)
-            add(n, jnp.dot(source[...], wq[pl.ds(base, width), lanes], preferred_element_type=f32))
-            return carry
-
-        def keyval(n, carry):
-            add(3 + n, jnp.dot(source[...], wkv[n, pl.ds(base, width), :], preferred_element_type=f32))
-            return carry
-
-        lax.fori_loop(0, 3, queries, 0)
-        lax.fori_loop(0, 2, keyval, 0)
+    def project_diag(i):
+        forward[i].wait_recv()
+        project(diag, i * size, size, False)
+
+    def project_opp(i):
+        project(opp, i * size, size, False)
 
     partner = peer(1)
     wanted = lax.shift_right_logical(prompt_ref[partner], 1)
 
     def pair(kind):
         return remote(
-            stage.at[kind], landed.at[kind], pair_send.at[kind], pair_recv.at[kind], (partner, tp)
+            stage.at[kind], landed.at[kind // 2, pl.ds((kind % 2) * part_len, part_len)],
+            pair_send.at[kind], pair_recv.at[kind], (partner, tp),
         )
 
     def hand_over(kind):
         receive(kind, 3)
         stage[kind] = bufs[kind][wanted]
         pair(kind).start()
-
-    advance(1, (0, 1, 2, 3))
-    loads[0].wait()
-    loads[1].wait()
-    project(tp, True)
-    relay(0)
-    advance(2, (0, 1))
-    relay(1)
-    to_sib.wait_recv()
-    project(sib, False)
-    advance(2, (2, 3))
-    relay(2)
-    hand_over(0)
-    hand_over(1)
 
     lane = lax.broadcasted_iota(jnp.int32, (1, count), 1)
     token = lax.rem(lane, RMAX)
@@ -311,13 +307,38 @@
     col = lax.broadcasted_iota(jnp.int32, (half, half), 1)
     causal = (lax.div(row, RMAX) == lax.div(col, RMAX)) & (row >= col)
 
-    relay(PIECES - 1)
-    project(opp, False)
+    for load in blocks[0]:
+        load.wait()
+    project(tp, 0, width, True)
+    advance(1, (0, 1, 2, 3))
+    relay(0)
+    to_sib.wait_recv()
+    for load in blocks[1]:
+        load.wait()
+    project(sib, 0, width, False)
+    relay(1)
+    advance(2, (0, 1))
+    for i in (2, 3):
+        for load in blocks[i]:
+            load.wait()
+    project_opp(0)
+    project_diag(0)
+    relay(2)
+    project_opp(1)
+    advance(2, (2, 3))
+    project_diag(1)
+    relay(3)
+    project_opp(2)
+    project_diag(2)
+    hand_over(0)
+    hand_over(1)
+    project_opp(3)
+    project_diag(3)
+    relay(4)
+    project_opp(4)
     hand_over(2)
     hand_over(3)
-    for i in range(PIECES):
-        forward[i].wait_recv()
-    project(diag, False)
+    project_diag(4)
 
     for table in tables:
         table.wait()
@@ -344,10 +365,13 @@
 
     def fetch(kind):
         pair(kind).wait_recv()
-        return jnp.where(here_too, bufs[kind][lax.shift_right_logical(mine, 1)], landed[kind])
+        part = slice((kind % 2) * part_len, (kind % 2 + 1) * part_len)
+        landed[kind // 2, part] = jnp.where(
+            here_too, bufs[kind][lax.shift_right_logical(mine, 1)], landed[kind // 2, part]
+        )
 
     for kind in range(4):
-        landed[kind] = fetch(kind)
+        fetch(kind)
 
     def attend_rows(base):
         span_rows = pl.ds(base, half)
@@ -358,38 +382,29 @@
             query = dealt[h // 2, span_rows, (h % 2) * HD:(h % 2 + 1) * HD]
             own_key = dealt[3, span_rows, lanes]
             own_value = dealt[4, span_rows, lanes]
-            first = lax.dot_general(query, landed[0, :, lanes], nt, preferred_element_type=f32)
-            second = lax.dot_general(query, landed[1, :, lanes], nt, preferred_element_type=f32)
-            recent = lax.dot_general(query, own_key, nt, preferred_element_type=f32) * scale
-            first, second = first * scale, second * scale
-            recent = jnp.where(causal, recent, -1e30)
-            top = jnp.max(
-                jnp.maximum(jnp.maximum(first, second), recent), -1, keepdims=True
+            prior = lax.dot_general(query, landed[0, :, lanes], nt, preferred_element_type=f32)
+            recent = lax.dot_general(query, own_key, nt, preferred_element_type=f32)
+            prior = prior * scale
+            recent = jnp.where(causal, recent * scale, -1e30)
+            top = jnp.maximum(
+                jnp.max(prior, -1, keepdims=True), jnp.max(recent, -1, keepdims=True)
             )
-            first, second = jnp.exp(first - top), jnp.exp(second - top)
-            recent = jnp.exp(recent - top)
-            share = mask / jnp.sum(first + second + recent, -1, keepdims=True)
-            mixed = (
-                jnp.dot((first * share).astype(bf16), landed[2, :, lanes],
-                        preferred_element_type=f32)
-                + jnp.dot((second * share).astype(bf16), landed[3, :, lanes],
-                          preferred_element_type=f32)
-                + jnp.dot((recent * share).astype(bf16), own_value, preferred_element_type=f32)
-            )
+            prior, recent = jnp.exp(prior - top), jnp.exp(recent - top)
+            total = jnp.sum(prior, -1, keepdims=True) + jnp.sum(recent, -1, keepdims=True)
+            share = mask / total
+            mixed = jnp.dot(
+                (prior * share).astype(bf16), landed[1, :, lanes], preferred_element_type=f32
+            ) + jnp.dot((recent * share).astype(bf16), own_value, preferred_element_type=f32)
             attn[span_rows, h * HD:(h + 1) * HD] = mixed.astype(bf16)
 
     def partial(owner, dst, base):
         span_rows = pl.ds(base, half)
 
-        def tile(n, carry):
+        for n in range(width // 256):
             source = pl.ds(pl.multiple_of(owner * width + n * 256, 256), 256)
-            lanes = pl.ds(pl.multiple_of(n * 256, 256), 256)
-            dst[span_rows, lanes] = jnp.dot(
+            dst[span_rows, n * 256:(n + 1) * 256] = jnp.dot(
                 attn[span_rows], wo[:, source], preferred_element_type=f32
             ).astype(bf16)
-            return carry
-
-        lax.fori_loop(0, width // 256, tile, 0)
 
     def swap(i, side):
         span_rows = pl.ds(bases[side], half)
@@ -440,7 +455,7 @@
         pl.multiple_of((1 - z // 2) * half, half),
         pl.multiple_of((z // 2) * half, half),
     )
-    loads[2].wait()
+    wo_load.wait()
     attend_rows(bases[0])
     partial(diag, queue.at[0], bases[0])
     swap(0, 0).start()
@@ -525,7 +540,7 @@
             pltpu.VMEM((4,) + cache, bf16),
             pltpu.VMEM((4,) + cache, bf16),
             pltpu.VMEM((4,) + cache, bf16),
-            pltpu.VMEM((4,) + cache, bf16),
+            pltpu.VMEM((2, PL, w_keyval.shape[2]), bf16),
             pltpu.VMEM((5, count, 256), bf16),
             pltpu.VMEM((count, HD), jnp.float32),
             pltpu.VMEM((count, w_query.shape[1]), bf16),
@@ -535,7 +550,7 @@
             pltpu.VMEM(block, bf16),
             pltpu.VMEM(block, bf16),
             pltpu.VMEM(block, bf16),
-            dma((10,)),
+            dma((16,)),
             dma((1 + 2 * PIECES,)),
             dma((1 + 2 * PIECES,)),
             dma((4, 2, 3)),

time: 59 us -> 57 us (0.966)
  Pallas kernels: 56.9 us -> 54.9 us
    pallas_call x1, Pallas kernels: 56.9 us -> 54.9 us  [fused_device(): pl.pallas_call(fused_kernel, out_shape=jax.ShapeDtypeStruct(block, bf16),...]
where the time goes in v4:
time: 57 us; the launch traced here: 56.9 us
  Pallas kernels  54.9 us (96%)
  local copies, waits for them, and re-layouts  1.97 us (3%)
    pallas_call x1, Pallas kernels, fused_device(): pl.pallas_call(fused_kernel, out_shape=jax.ShapeDtypeStruct(block, bf16),...  54.9 us
    unnamed x1, local copies, waits for them, and re-layouts  1.97 us

profile of v4, /device:TPU:0, one launch (start us, length us, event | category | flops | bytes accessed | tf_op | source)
XLA Modules:
  0.0 56.9 jit_solution(6118667851489684665)
XLA Ops:
  0.0 54.9 %shard_map.100 = bf16[256,1280]{1,0:T(8,128)(2,1)} custom-call(s32[128]{0:T(128)} %bitcast.7, s32[128]{0:T(128)} %len_ref.1, s32[8]{0:T(128)} %prompt_ref.1, f32[16,128]{1,0:T(8,128)} %constant.4.clone.cos_hbm, f32[16,128]{1,0:T(8,128)} %constant.5.clone.sin_hbm, bf16[256,1280]{1,0:T(8,128)(2,1)} %bitcast.5, bf16[2,256,256]{2,1,0:T(8,128)(2,1)} %bitcast.6, ...), custom_call_target="tpu_custom_call" | custom-call | flops 6000000000 | bytes 23000000 | tf_op jit(solution)/shard_map/pallas_call | solution.py:525
  54.9 2.0 %copy.12 = bf16[16,16,1280]{2,1,0:T(8,128)(2,1)} copy(bf16[16,16,1280]{2,1,0:T(8,128)(2,1)} %bitcast.4) | data formatting | bytes 1310720

commit v5 on v4

--- a/solution.py
+++ b/solution.py
@@ -166,10 +166,15 @@
     wo_load = local(wo_hbm, wo, 15)
     for load in [x_load] + kv_loads + tables:
         load.start()
-    for block in blocks:
-        for load in block:
+    def begin(i):
+        for load in blocks[i]:
             load.start()
-    wo_load.start()
+
+    def ready(i):
+        for load in blocks[i]:
+            load.wait()
+
+    begin(0)
 
     barrier = pltpu.get_barrier_semaphore()
     for m in range(1, 8):
@@ -239,6 +244,7 @@
         kv_loads[kind].wait()
         launch(kind, 0)
     to_sib.start()
+    begin(1)
 
     def advance(step, kinds):
         for kind in kinds:
@@ -307,20 +313,20 @@
     col = lax.broadcasted_iota(jnp.int32, (half, half), 1)
     causal = (lax.div(row, RMAX) == lax.div(col, RMAX)) & (row >= col)
 
-    for load in blocks[0]:
-        load.wait()
+    ready(0)
+    begin(2)
     project(tp, 0, width, True)
     advance(1, (0, 1, 2, 3))
     relay(0)
     to_sib.wait_recv()
-    for load in blocks[1]:
-        load.wait()
+    ready(1)
+    begin(3)
     project(sib, 0, width, False)
     relay(1)
     advance(2, (0, 1))
-    for i in (2, 3):
-        for load in blocks[i]:
-            load.wait()
+    ready(2)
+    ready(3)
+    wo_load.start()
     project_opp(0)
     project_diag(0)
     relay(2)

time: 57 us -> 57 us (level)
  no operation moved by 1% of the time
where the time goes in v5:
time: 57 us; the launch traced here: 56.9 us
  Pallas kernels  54.9 us (96%)
  local copies, waits for them, and re-layouts  1.97 us (3%)
    pallas_call x1, Pallas kernels, fused_device(): pl.pallas_call(fused_kernel, out_shape=jax.ShapeDtypeStruct(block, bf16),...  54.9 us
    unnamed x1, local copies, waits for them, and re-layouts  1.97 us

profile of v5, /device:TPU:0, one launch (start us, length us, event | category | flops | bytes accessed | tf_op | source)
XLA Modules:
  0.0 56.9 jit_solution(4336891116473759534)
XLA Ops:
  0.0 54.9 %shard_map.100 = bf16[256,1280]{1,0:T(8,128)(2,1)} custom-call(s32[128]{0:T(128)} %bitcast.7, s32[128]{0:T(128)} %len_ref.1, s32[8]{0:T(128)} %prompt_ref.1, f32[16,128]{1,0:T(8,128)} %constant.4.clone.cos_hbm, f32[16,128]{1,0:T(8,128)} %constant.5.clone.sin_hbm, bf16[256,1280]{1,0:T(8,128)(2,1)} %bitcast.5, bf16[2,256,256]{2,1,0:T(8,128)(2,1)} %bitcast.6, ...), custom_call_target="tpu_custom_call" | custom-call | flops 6000000000 | bytes 23000000 | tf_op jit(solution)/shard_map/pallas_call | solution.py:531
  54.9 2.0 %copy.12 = bf16[16,16,1280]{2,1,0:T(8,128)(2,1)} copy(bf16[16,16,1280]{2,1,0:T(8,128)(2,1)} %bitcast.4) | data formatting | bytes 1310720

commit v6 on v4

--- a/solution.py
+++ b/solution.py
@@ -126,7 +126,7 @@
 def fused_kernel(
     shard_ref, len_ref, prompt_ref, cos_hbm, sin_hbm, x_hbm, kv_hbm, wq_hbm, wkv_hbm, wo_hbm,
     out_ref,
-    wq, wkv, wo, rows, acc, cos_ref, sin_ref, buf0, buf1, buf2, buf3, stage, landed, dealt, valid,
+    wq, wkv, wo, rows, acc, cos_ref, sin_ref, buf0, buf1, buf2, buf3, stage, landed, stacked, own, valid,
     attn, queue, sibling, ahead, kept, across, done,
     load_sem, gather_send, gather_recv, line_send, line_recv, pair_send, pair_recv,
     sib_send, sib_recv, cross_send, cross_recv, out_send, out_recv,
@@ -235,7 +235,7 @@
     x_load.wait()
     for copy in to_opp:
         copy.start()
-    for kind in range(4):
+    for kind in (0, 1):
         kv_loads[kind].wait()
         launch(kind, 0)
     to_sib.start()
@@ -310,7 +310,10 @@
     for load in blocks[0]:
         load.wait()
     project(tp, 0, width, True)
-    advance(1, (0, 1, 2, 3))
+    advance(1, (0, 1))
+    for kind in (2, 3):
+        kv_loads[kind].wait()
+        launch(kind, 0)
     relay(0)
     to_sib.wait_recv()
     for load in blocks[1]:
@@ -322,16 +325,17 @@
         for load in blocks[i]:
             load.wait()
     project_opp(0)
+    advance(1, (2, 3))
     project_diag(0)
     relay(2)
+    hand_over(0)
+    hand_over(1)
     project_opp(1)
+    project_diag(1)
     advance(2, (2, 3))
-    project_diag(1)
     relay(3)
     project_opp(2)
     project_diag(2)
-    hand_over(0)
-    hand_over(1)
     project_opp(3)
     project_diag(3)
     relay(4)
@@ -356,11 +360,20 @@
             tile = jnp.concatenate([turn(acc[n, :, :HD]), turn(acc[n, :, HD:])], -1)
         else:
             tile = acc[n].astype(bf16)
-        dealt[n] = jnp.dot(deal, tile, preferred_element_type=f32).astype(bf16)
+        tile = jnp.dot(deal, tile, preferred_element_type=f32).astype(bf16)
+        for side in (0, 1):
+            part = tile[side * half:(side + 1) * half]
+            if n >= 3:
+                own[n - 3, side] = part
+                continue
+            for j in (0, 1):
+                head = 2 * n + j
+                place_of = slice((head % 3) * half, (head % 3 + 1) * half)
+                stacked[head // 3, side, place_of] = part[:, j * HD:(j + 1) * HD]
 
     mine = prompt_ref[seq]
     here_too = lax.rem(mine, 2) == x
-    scale = 1.0 / math.sqrt(HD)
+    rate = math.log2(math.e) / math.sqrt(HD)
     nt = (((1,), (1,)), ((), ()))
 
     def fetch(kind):
@@ -370,32 +383,37 @@
             here_too, bufs[kind][lax.shift_right_logical(mine, 1)], landed[kind // 2, part]
         )
 
-    for kind in range(4):
-        fetch(kind)
-
-    def attend_rows(base):
-        span_rows = pl.ds(base, half)
-        mask = valid[span_rows, :1]
-        for h in range(6):
-            k = h // 3
-            lanes = slice(k * HD, (k + 1) * HD)
-            query = dealt[h // 2, span_rows, (h % 2) * HD:(h % 2 + 1) * HD]
-            own_key = dealt[3, span_rows, lanes]
-            own_value = dealt[4, span_rows, lanes]
-            prior = lax.dot_general(query, landed[0, :, lanes], nt, preferred_element_type=f32)
-            recent = lax.dot_general(query, own_key, nt, preferred_element_type=f32)
-            prior = prior * scale
-            recent = jnp.where(causal, recent * scale, -1e30)
-            top = jnp.maximum(
-                jnp.max(prior, -1, keepdims=True), jnp.max(recent, -1, keepdims=True)
+    def weigh(side, base, k):
+        lanes = slice(k * HD, (k + 1) * HD)
+        queries = stacked[k, side]
+        prior_all = lax.dot_general(queries, landed[0, :, lanes], nt, preferred_element_type=f32)
+        recent_all = lax.dot_general(queries, own[0, side, :, lanes], nt, preferred_element_type=f32)
+        mask = valid[pl.ds(base, half), :1]
+        priors, recents, shares = [], [], []
+        for r in range(3):
+            prior = prior_all[r * half:(r + 1) * half]
+            recent = jnp.where(causal, recent_all[r * half:(r + 1) * half], -1e30)
+            top = jnp.max(
+                jnp.maximum(jnp.maximum(prior[:, :HD], prior[:, HD:]), recent), -1, keepdims=True
             )
-            prior, recent = jnp.exp(prior - top), jnp.exp(recent - top)
-            total = jnp.sum(prior, -1, keepdims=True) + jnp.sum(recent, -1, keepdims=True)
-            share = mask / total
-            mixed = jnp.dot(
-                (prior * share).astype(bf16), landed[1, :, lanes], preferred_element_type=f32
-            ) + jnp.dot((recent * share).astype(bf16), own_value, preferred_element_type=f32)
-            attn[span_rows, h * HD:(h + 1) * HD] = mixed.astype(bf16)
+            prior = jnp.exp2((prior - top) * rate)
+            recent = jnp.exp2((recent - top) * rate)
+            total = jnp.sum(prior[:, :HD] + prior[:, HD:] + recent, -1, keepdims=True)
+            priors.append(prior.astype(bf16))
+            recents.append(recent.astype(bf16))
+            shares.append(mask / total)
+        return jnp.concatenate(priors, 0), jnp.concatenate(recents, 0), shares
+
+    def mix(side, base, k, weights):
+        lanes = slice(k * HD, (k + 1) * HD)
+        priors, recents, shares = weights
+        mixed = jnp.dot(priors, landed[1, :, lanes], preferred_element_type=f32)
+        mixed = mixed + jnp.dot(recents, own[1, side, :, lanes], preferred_element_type=f32)
+        for r in range(3):
+            head = 3 * k + r
+            attn[pl.ds(base, half), head * HD:(head + 1) * HD] = (
+                mixed[r * half:(r + 1) * half] * shares[r]
+            ).astype(bf16)
 
     def partial(owner, dst, base):
         span_rows = pl.ds(base, half)
@@ -455,8 +473,16 @@
         pl.multiple_of((1 - z // 2) * half, half),
         pl.multiple_of((z // 2) * half, half),
     )
+    sides = (1 - z // 2, z // 2)
+    fetch(0)
+    fetch(1)
+    first = weigh(sides[0], bases[0], 0)
+    second = weigh(sides[0], bases[0], 1)
+    fetch(2)
+    fetch(3)
+    mix(sides[0], bases[0], 0, first)
+    mix(sides[0], bases[0], 1, second)
     wo_load.wait()
-    attend_rows(bases[0])
     partial(diag, queue.at[0], bases[0])
     swap(0, 0).start()
     partial(opp, ahead, bases[0])
@@ -466,21 +492,22 @@
     for m in ORDER[:4]:
         pass_on(m)
     partial(tp, kept, bases[0])
-    attend_rows(bases[1])
+    mix(sides[1], bases[1], 0, weigh(sides[1], bases[1], 0))
     swap(1, 0).wait_recv()
     finish(ORDER[0])
+    mix(sides[1], bases[1], 1, weigh(sides[1], bases[1], 1))
+    finish(ORDER[1])
     partial(diag, queue.at[0], bases[1])
     swap(0, 1).start()
     partial(opp, ahead, bases[1])
-    partial(sib, queue.at[1], bases[1])
-    swap(1, 1).start()
+    finish(ORDER[2])
     swap(0, 1).wait_recv()
     for m in ORDER[4:]:
         pass_on(m)
-    finish(ORDER[1])
+    finish(ORDER[3])
+    partial(sib, queue.at[1], bases[1])
+    swap(1, 1).start()
     partial(tp, kept, bases[1])
-    finish(ORDER[2])
-    finish(ORDER[3])
     swap(1, 1).wait_recv()
     for m in ORDER[4:]:
         finish(m)
@@ -541,7 +568,8 @@
             pltpu.VMEM((4,) + cache, bf16),
             pltpu.VMEM((4,) + cache, bf16),
             pltpu.VMEM((2, PL, w_keyval.shape[2]), bf16),
-            pltpu.VMEM((5, count, 256), bf16),
+            pltpu.VMEM((2, 2, 3 * count // 2, HD), bf16),
+            pltpu.VMEM((2, 2, count // 2, 256), bf16),
             pltpu.VMEM((count, HD), jnp.float32),
             pltpu.VMEM((count, w_query.shape[1]), bf16),
             pltpu.VMEM((2,) + block, bf16),

time: 57 us -> 56.5 us (level)
  no operation moved by 1% of the time
where the time goes in v6:
time: 56.5 us; the launch traced here: 56.4 us
  Pallas kernels  54.4 us (96%)
  local copies, waits for them, and re-layouts  1.97 us (3%)
    pallas_call x1, Pallas kernels, fused_device(): pl.pallas_call(fused_kernel, out_shape=jax.ShapeDtypeStruct(block, bf16),...  54.4 us
    unnamed x1, local copies, waits for them, and re-layouts  1.97 us

profile of v6, /device:TPU:0, one launch (start us, length us, event | category | flops | bytes accessed | tf_op | source)
XLA Modules:
  0.0 56.4 jit_solution(10639505102470775589)
XLA Ops:
  0.0 54.4 %shard_map.100 = bf16[256,1280]{1,0:T(8,128)(2,1)} custom-call(s32[128]{0:T(128)} %bitcast.7, s32[128]{0:T(128)} %len_ref.1, s32[8]{0:T(128)} %prompt_ref.1, f32[16,128]{1,0:T(8,128)} %constant.4.clone.cos_hbm, f32[16,128]{1,0:T(8,128)} %constant.5.clone.sin_hbm, bf16[256,1280]{1,0:T(8,128)(2,1)} %bitcast.5, bf16[2,256,256]{2,1,0:T(8,128)(2,1)} %bitcast.6, ...), custom_call_target="tpu_custom_call" | custom-call | flops 6000000000 | bytes 23000000 | tf_op jit(solution)/shard_map/pallas_call | solution.py:552
  54.4 2.0 %copy.12 = bf16[16,16,1280]{2,1,0:T(8,128)(2,1)} copy(bf16[16,16,1280]{2,1,0:T(8,128)(2,1)} %bitcast.4) | data formatting | bytes 1310720

commit v7 on v6

--- a/solution.py
+++ b/solution.py
@@ -492,19 +492,19 @@
     for m in ORDER[:4]:
         pass_on(m)
     partial(tp, kept, bases[0])
-    mix(sides[1], bases[1], 0, weigh(sides[1], bases[1], 0))
     swap(1, 0).wait_recv()
     finish(ORDER[0])
+    mix(sides[1], bases[1], 0, weigh(sides[1], bases[1], 0))
+    finish(ORDER[1])
     mix(sides[1], bases[1], 1, weigh(sides[1], bases[1], 1))
-    finish(ORDER[1])
+    finish(ORDER[2])
     partial(diag, queue.at[0], bases[1])
     swap(0, 1).start()
+    finish(ORDER[3])
     partial(opp, ahead, bases[1])
-    finish(ORDER[2])
     swap(0, 1).wait_recv()
     for m in ORDER[4:]:
         pass_on(m)
-    finish(ORDER[3])
     partial(sib, queue.at[1], bases[1])
     swap(1, 1).start()
     partial(tp, kept, bases[1])

time: 56.5 us -> 57.8 us (1.023)
  Pallas kernels: 54.4 us -> 55.6 us
    pallas_call x1, Pallas kernels: 54.4 us -> 55.6 us  [fused_device(): pl.pallas_call(fused_kernel, out_shape=jax.ShapeDtypeStruct(block, bf16),...]
where the time goes in v7:
time: 57.8 us; the launch traced here: 57.6 us
  Pallas kernels  55.6 us (96%)
  local copies, waits for them, and re-layouts  1.97 us (3%)
    pallas_call x1, Pallas kernels, fused_device(): pl.pallas_call(fused_kernel, out_shape=jax.ShapeDtypeStruct(block, bf16),...  55.6 us
    unnamed x1, local copies, waits for them, and re-layouts  1.97 us

profile of v7, /device:TPU:0, one launch (start us, length us, event | category | flops | bytes accessed | tf_op | source)
XLA Modules:
  0.0 57.6 jit_solution(14462587217283339003)
XLA Ops:
  0.0 55.6 %shard_map.100 = bf16[256,1280]{1,0:T(8,128)(2,1)} custom-call(s32[128]{0:T(128)} %bitcast.7, s32[128]{0:T(128)} %len_ref.1, s32[8]{0:T(128)} %prompt_ref.1, f32[16,128]{1,0:T(8,128)} %constant.4.clone.cos_hbm, f32[16,128]{1,0:T(8,128)} %constant.5.clone.sin_hbm, bf16[256,1280]{1,0:T(8,128)(2,1)} %bitcast.5, bf16[2,256,256]{2,1,0:T(8,128)(2,1)} %bitcast.6, ...), custom_call_target="tpu_custom_call" | custom-call | flops 6000000000 | bytes 23000000 | tf_op jit(solution)/shard_map/pallas_call | solution.py:552
  55.6 2.0 %copy.12 = bf16[16,16,1280]{2,1,0:T(8,128)(2,1)} copy(bf16[16,16,1280]{2,1,0:T(8,128)(2,1)} %bitcast.4) | data formatting | bytes 1310720
